TPU v7x, 128 devices: a whole 4x4x4 slice. The times are simulated.
128 devices in a mesh: ctx: 16 (over z_hi, x, core), exp: 8 (over y, z_lo).
Axes of the slice: x: 4, y: 4, z: 4 (z_hi: 2, z_lo: 2; z = z_hi * 2 + z_lo), core: 2. Of those that a mesh axis runs over, the one named last changes fastest.
Arguments:
- queries: bfloat16 [6144, 4096], P('ctx', 'exp'), may hold values from -24 to 24
- keys: bfloat16 [6144, 256], P('ctx'), may hold values from -12 to 12
- values: bfloat16 [6144, 256], P('ctx'), may hold values from -6 to 6
- out_grad: bfloat16 [6144, 4096], P('ctx', 'exp'), may hold values from -6 to 6
- moe_grad: bfloat16 [16384, 4096], P(('ctx', 'exp')), may hold values from -4 to 4
- expert_ids: int32 [16384, 8], P(('ctx', 'exp')), may hold values from 0 to 127, as said below
- gate_weights: bfloat16 [16384, 8], P(('ctx', 'exp')), may hold values from 0.19921875 to 1
- saved_gate: bfloat16 [16384, 1536], P(('ctx', 'exp')), may hold values from -6 to 6
- saved_up: bfloat16 [16384, 1536], P(('ctx', 'exp')), may hold values from -6 to 6
- down_weight: bfloat16 [8, 1536, 4096], P('exp'), may hold values from -0.15625 to 0.15625
Outputs:
- query_grad: bfloat16 [6144, 4096], P('ctx', 'exp')
- key_grad: bfloat16 [6144, 256], P(('ctx', 'exp'))
- value_grad: bfloat16 [6144, 256], P(('ctx', 'exp'))
- gate_grad: float32 [16384, 8], P(('ctx', 'exp'))
- gate_pre_grad: bfloat16 [16384, 1536], P(('ctx', 'exp'))
- up_pre_grad: bfloat16 [16384, 1536], P(('ctx', 'exp'))
Inputs may be any that keep to these rules, and one draw needn't show every extreme that they name: `expert_ids`: each row names 8 different experts. In each aligned block of 128 rows (the rows of one device) no expert is named by more than 16 rows, and some expert below 8 is named by exactly 16 rows; in the blocks c * 8 to c * 8 + 7 that is the same expert.
All inputs are finite; a program needn't handle non-finite values.
Results may differ from a plain program's by a relative error of at most 0.0052.
Values may be sent and summed in bfloat16 or wider, within the bound.
A program may use at most 128 MiB of HBM per device.

v0:
```python
import jax
import jax.numpy as jnp
from jax import lax
from jax.sharding import PartitionSpec as P

QHEADS = 32
KVHEADS = 2
HEAD = 128
TOPK = 8
CAP = 16


def passed_along(block, axis, distance):
    devices = range(lax.axis_size(axis))
    route = [((i - distance) % len(devices), i) for i in devices]
    return lax.ppermute(block, axis, route)


def tile_scores(query_half, grad_half, kv_half):
    key_part = kv_half[:, :HEAD]
    value_part = kv_half[:, HEAD:]
    scores = jnp.einsum(
        "qhd,kd->hqk", query_half, key_part, preferred_element_type=jnp.float32
    ) * HEAD ** (-0.5)
    prob_grad = jnp.einsum("qhd,kd->hqk", grad_half, value_part, preferred_element_type=jnp.float32)
    return (scores, prob_grad)


def half_mask(query_half_id, key_half_id, half_rows):
    offsets = jnp.arange(half_rows, dtype=jnp.int32)
    return (query_half_id * half_rows + offsets)[:, None] >= (key_half_id * half_rows + offsets)[
        None, :
    ]


def tile_stats(statistics, query_half, grad_half, kv_half, visible):
    running_max, exp_total, weighted = statistics
    scores, prob_grad = tile_scores(query_half, grad_half, kv_half)
    scores = jnp.where(visible[None], scores, -jnp.inf)
    new_max = jnp.maximum(running_max, jnp.max(scores, axis=2))
    factor = jnp.exp(running_max - new_max)
    exponent = jnp.exp(scores - new_max[:, :, None])
    exp_total = exp_total * factor + jnp.sum(exponent, axis=2)
    weighted = weighted * factor + jnp.sum(exponent * prob_grad, axis=2)
    return (new_max, exp_total, weighted)


def tile_grads(query_half, grad_half, kv_half, visible, log_total, row_delta):
    scores, prob_grad = tile_scores(query_half, grad_half, kv_half)
    scores = jnp.where(visible[None], scores, -jnp.inf)
    probabilities = jnp.exp(scores - log_total[:, :, None])
    score_grad = probabilities * (prob_grad - row_delta[:, :, None])
    probs_b = probabilities.astype(jnp.bfloat16)
    score_b = score_grad.astype(jnp.bfloat16)
    score_scale = HEAD ** (-0.5)
    query_grad = (
        jnp.einsum("hqk,kd->qhd", score_b, kv_half[:, :HEAD], preferred_element_type=jnp.float32)
        * score_scale
    )
    key_grad = (
        jnp.einsum("hqk,qhd->kd", score_b, query_half, preferred_element_type=jnp.float32)
        * score_scale
    )
    value_grad = jnp.einsum("hqk,qhd->kd", probs_b, grad_half, preferred_element_type=jnp.float32)
    return (query_grad, jnp.concatenate([key_grad, value_grad], axis=1))


def apply_stats(operands):
    return tile_stats(*operands)


def skip_stats(operands):
    return operands[0]


def apply_grads(operands):
    return tile_grads(*operands)


def skip_grads(operands):
    return (jnp.zeros(operands[0].shape, jnp.float32), jnp.zeros(operands[2].shape, jnp.float32))


def block_stats(statistics, query_halves, grad_halves, kv_block, query_ids, key_ids):
    half_rows = kv_block.shape[0] // 2
    updated = []
    for query_side in range(2):
        current = statistics[query_side]
        for key_side in range(2):
            kv_half = kv_block[key_side * half_rows : (key_side + 1) * half_rows]
            visible = half_mask(query_ids[query_side], key_ids[key_side], half_rows)
            operands = (
                current,
                query_halves[query_side],
                grad_halves[query_side],
                kv_half,
                visible,
            )
            current = lax.cond(
                query_ids[query_side] >= key_ids[key_side], apply_stats, skip_stats, operands
            )
        updated.append(current)
    return tuple(updated)


def block_grads(query_halves, grad_halves, kv_block, query_ids, key_ids, finals):
    half_rows = kv_block.shape[0] // 2
    query_terms = []
    pair_terms = [
        jnp.zeros((half_rows, kv_block.shape[1]), jnp.float32),
        jnp.zeros((half_rows, kv_block.shape[1]), jnp.float32),
    ]
    for query_side in range(2):
        query_term = jnp.zeros(query_halves[query_side].shape, jnp.float32)
        log_total, row_delta = finals[query_side]
        for key_side in range(2):
            kv_half = kv_block[key_side * half_rows : (key_side + 1) * half_rows]
            visible = half_mask(query_ids[query_side], key_ids[key_side], half_rows)
            operands = (
                query_halves[query_side],
                grad_halves[query_side],
                kv_half,
                visible,
                log_total,
                row_delta,
            )
            query_piece, pair_piece = lax.cond(
                query_ids[query_side] >= key_ids[key_side], apply_grads, skip_grads, operands
            )
            query_term = query_term + query_piece
            pair_terms[key_side] = pair_terms[key_side] + pair_piece
        query_terms.append(query_term)
    return (jnp.stack(query_terms), jnp.concatenate(pair_terms, axis=0))


def finish(statistics):
    running_max, exp_total, weighted = statistics
    return (running_max + jnp.log(exp_total), weighted / exp_total)


def empty_stats(head_count, half_rows):
    return (
        jnp.full((head_count, half_rows), -jnp.inf, jnp.float32),
        jnp.zeros((head_count, half_rows), jnp.float32),
        jnp.zeros((head_count, half_rows), jnp.float32),
    )


def shards(
    queries,
    keys,
    values,
    out_grad,
    moe_grad,
    expert_ids,
    gate_weights,
    saved_gate,
    saved_up,
    down_weight,
):
    own_index = lax.axis_index("ctx")
    cycle_size = lax.axis_size("ctx")
    local_rows = queries.shape[0]
    half_rows = local_rows // 2
    column_count = queries.shape[1]
    head_count = column_count // HEAD
    kv_head = lax.axis_index("exp") * head_count // (QHEADS // KVHEADS)
    key_value = jnp.concatenate(
        [
            lax.dynamic_slice_in_dim(keys, kv_head * HEAD, HEAD, 1),
            lax.dynamic_slice_in_dim(values, kv_head * HEAD, HEAD, 1),
        ],
        axis=1,
    )

    def half_ids(device):
        return jnp.stack([2 * device, 2 * device + 1])

    query_halves = queries.reshape(2, half_rows, head_count, HEAD)
    grad_halves = out_grad.reshape(2, half_rows, head_count, HEAD)
    query_ids = half_ids(own_index)
    start_stats = (empty_stats(head_count, half_rows), empty_stats(head_count, half_rows))
    zero_query = jnp.zeros((2, half_rows, head_count, HEAD), jnp.float32)

    def rotate(kv_block):
        return passed_along(kv_block, "ctx", 1)

    def stats_step(turn_index, loop_state):
        statistics, kv_block = loop_state
        source = (own_index - turn_index) % cycle_size
        statistics = block_stats(
            statistics, query_halves, grad_halves, kv_block, query_ids, half_ids(source)
        )
        return (statistics, rotate(kv_block))

    statistics, kv_home = lax.fori_loop(0, cycle_size, stats_step, (start_stats, key_value))
    finals = (finish(statistics[0]), finish(statistics[1]))

    def grad_step(turn_index, loop_state):
        query_acc, kv_block, pair_acc = loop_state
        source = (own_index - turn_index) % cycle_size
        query_term, pair_term = block_grads(
            query_halves, grad_halves, kv_block, query_ids, half_ids(source), finals
        )
        return (
            query_acc + query_term,
            rotate(kv_block),
            passed_along(pair_acc + pair_term, "ctx", 1),
        )

    query_acc, kv_after, pair_acc = lax.fori_loop(
        0,
        cycle_size,
        grad_step,
        (zero_query, kv_home, jnp.zeros((local_rows, 2 * HEAD), jnp.float32)),
    )
    query_flat = query_acc.reshape(local_rows, column_count)
    columns = KVHEADS * HEAD
    key_full = lax.dynamic_update_slice_in_dim(
        jnp.zeros((local_rows, columns), jnp.float32), pair_acc[:, :HEAD], kv_head * HEAD, 1
    )
    value_full = lax.dynamic_update_slice_in_dim(
        jnp.zeros((local_rows, columns), jnp.float32), pair_acc[:, HEAD:], kv_head * HEAD, 1
    )
    key_sum, value_sum = (
        lax.psum_scatter(key_full, "exp", scatter_dimension=0, tiled=True),
        lax.psum_scatter(value_full, "exp", scatter_dimension=0, tiled=True),
    )
    query_grad = query_flat.astype(jnp.bfloat16)
    group_size = lax.axis_size("exp")
    token_count = moe_grad.shape[0]
    route_count = token_count * TOPK
    route_ids = expert_ids.reshape(-1)
    matches = (route_ids[:, None] == jnp.arange(group_size, dtype=jnp.int32)[None, :]).astype(
        jnp.int32
    )
    earlier = jnp.cumsum(matches, axis=0) - matches
    slot_rank = jnp.sum(earlier * matches, axis=1)
    in_flight = route_ids < group_size
    slot_total = group_size * CAP
    target_slot = jnp.where(in_flight, route_ids * CAP + slot_rank, slot_total)
    route_of = (
        jnp.zeros((slot_total + 1,), jnp.int32)
        .at[target_slot]
        .set(jnp.arange(route_count, dtype=jnp.int32))[:slot_total]
    )
    filled = jnp.zeros((slot_total + 1,), jnp.bool_).at[target_slot].set(True)[:slot_total]
    token_row = route_of // TOPK
    sent_rows = jnp.where(filled[:, None], moe_grad[token_row], jnp.zeros((), jnp.bfloat16))
    sent_weight = jnp.where(filled, gate_weights.reshape(-1)[route_of], jnp.zeros((), jnp.bfloat16))
    recv_rows, recv_weight = (
        lax.all_to_all(
            sent_rows.reshape(group_size, CAP, -1), "exp", split_axis=0, concat_axis=0, tiled=True
        ),
        lax.all_to_all(
            sent_weight.reshape(group_size, CAP), "exp", split_axis=0, concat_axis=0, tiled=True
        ),
    )
    recv_rows = recv_rows.reshape(slot_total, -1)
    recv_weight = recv_weight.reshape(-1).astype(jnp.float32)
    gate_f = saved_gate.astype(jnp.float32)
    up_f = saved_up.astype(jnp.float32)
    sigmoid_gate = jax.nn.sigmoid(gate_f)
    activation = (gate_f * sigmoid_gate * up_f).astype(jnp.bfloat16)
    expert_weight = down_weight[0]
    expert_out = jnp.dot(activation, expert_weight, preferred_element_type=jnp.float32)
    route_score = jnp.sum(recv_rows.astype(jnp.float32) * expert_out, axis=1)
    back_grad = lax.dot_general(
        recv_rows, expert_weight, (((1,), (1,)), ((), ())), preferred_element_type=jnp.float32
    )
    act_grad = recv_weight[:, None] * back_grad
    gate_pre_grad = (act_grad * up_f * sigmoid_gate * (1.0 + gate_f * (1.0 - sigmoid_gate))).astype(
        jnp.bfloat16
    )
    up_pre_grad = (act_grad * gate_f * sigmoid_gate).astype(jnp.bfloat16)
    returned = lax.all_to_all(
        route_score.reshape(group_size, CAP), "exp", split_axis=0, concat_axis=0, tiled=True
    ).reshape(-1)
    gate_grad = jnp.where(
        in_flight, returned[jnp.minimum(target_slot, slot_total - 1)], 0.0
    ).reshape(token_count, TOPK)
    return (
        query_grad,
        key_sum.astype(jnp.bfloat16),
        value_sum.astype(jnp.bfloat16),
        gate_grad,
        gate_pre_grad,
        up_pre_grad,
    )


def solution(mesh):
    in_specs = (
        P("ctx", "exp"),
        P("ctx", None),
        P("ctx", None),
        P("ctx", "exp"),
        P(("ctx", "exp"), None),
        P(("ctx", "exp"), None),
        P(("ctx", "exp"), None),
        P(("ctx", "exp"), None),
        P(("ctx", "exp"), None),
        P("exp", None, None),
    )
    out_specs = (
        P("ctx", "exp"),
        P(("ctx", "exp"), None),
        P(("ctx", "exp"), None),
        P(("ctx", "exp"), None),
        P(("ctx", "exp"), None),
        P(("ctx", "exp"), None),
    )
    return jax.shard_map(shards, mesh=mesh, in_specs=in_specs, out_specs=out_specs, check_vma=False)
```

profile of v0, /device:TPU:0, one launch (start us, length us, event | category | flops | bytes accessed | tf_op | source)
XLA Modules:
  0.0 789.2 jit_solution(6581698135628880275)
XLA Ops:
  11.4 156.1 %while.47 = (s32[]{:T(128)}, f32[4,192]{1,0:T(4,128)S(1)}, f32[4,192]{1,0:T(4,128)S(1)}, f32[4,192]{1,0:T(4,128)S(1)}, f32[4,192]{1,0:T(4,128)S(1)}, /*index=5*/...) while((s32[]{:T(128)}, f32[4,192]{1,0:T(4,128)S(1)}, ...), condition=%wide.region_21.22_spmd, body=%wide.region_0.21_spmd.sunk | while | flops 306865920 | bytes 13996414 | solution.py:196
  22.8 8.3 %collective-permute-done = bf16[384,256]{1,0:T(8,128)(2,1)} collective-permute-done((bf16[384,256]{1,0:T(8,128)(2,1)S(1)}, bf16[384,256]{1,0:T(8,128)(2,1)}, u32[]{:S(2)}, u32[]{:S(2)}) %collective-permute-start) | collective-permute-done | bytes 196640 | tf_op jit(solution)/shard_map/while/body/eval_jaxpr/ppermute | solution.py:16
  32.5 8.3 %collective-permute-done = bf16[384,256]{1,0:T(8,128)(2,1)} collective-permute-done((bf16[384,256]{1,0:T(8,128)(2,1)S(1)}, bf16[384,256]{1,0:T(8,128)(2,1)}, u32[]{:S(2)}, u32[]{:S(2)}) %collective-permute-start) | collective-permute-done | bytes 196640 | tf_op jit(solution)/shard_map/while/body/eval_jaxpr/ppermute | solution.py:16
  42.3 8.3 %collective-permute-done = bf16[384,256]{1,0:T(8,128)(2,1)} collective-permute-done((bf16[384,256]{1,0:T(8,128)(2,1)S(1)}, bf16[384,256]{1,0:T(8,128)(2,1)}, u32[]{:S(2)}, u32[]{:S(2)}) %collective-permute-start) | collective-permute-done | bytes 196640 | tf_op jit(solution)/shard_map/while/body/eval_jaxpr/ppermute | solution.py:16
  52.0 8.3 %collective-permute-done = bf16[384,256]{1,0:T(8,128)(2,1)} collective-permute-done((bf16[384,256]{1,0:T(8,128)(2,1)S(1)}, bf16[384,256]{1,0:T(8,128)(2,1)}, u32[]{:S(2)}, u32[]{:S(2)}) %collective-permute-start) | collective-permute-done | bytes 196640 | tf_op jit(solution)/shard_map/while/body/eval_jaxpr/ppermute | solution.py:16
  61.7 8.3 %collective-permute-done = bf16[384,256]{1,0:T(8,128)(2,1)} collective-permute-done((bf16[384,256]{1,0:T(8,128)(2,1)S(1)}, bf16[384,256]{1,0:T(8,128)(2,1)}, u32[]{:S(2)}, u32[]{:S(2)}) %collective-permute-start) | collective-permute-done | bytes 196640 | tf_op jit(solution)/shard_map/while/body/eval_jaxpr/ppermute | solution.py:16
  71.5 8.3 %collective-permute-done = bf16[384,256]{1,0:T(8,128)(2,1)} collective-permute-done((bf16[384,256]{1,0:T(8,128)(2,1)S(1)}, bf16[384,256]{1,0:T(8,128)(2,1)}, u32[]{:S(2)}, u32[]{:S(2)}) %collective-permute-start) | collective-permute-done | bytes 196640 | tf_op jit(solution)/shard_map/while/body/eval_jaxpr/ppermute | solution.py:16
  81.2 8.3 %collective-permute-done = bf16[384,256]{1,0:T(8,128)(2,1)} collective-permute-done((bf16[384,256]{1,0:T(8,128)(2,1)S(1)}, bf16[384,256]{1,0:T(8,128)(2,1)}, u32[]{:S(2)}, u32[]{:S(2)}) %collective-permute-start) | collective-permute-done | bytes 196640 | tf_op jit(solution)/shard_map/while/body/eval_jaxpr/ppermute | solution.py:16
  91.0 8.3 %collective-permute-done = bf16[384,256]{1,0:T(8,128)(2,1)} collective-permute-done((bf16[384,256]{1,0:T(8,128)(2,1)S(1)}, bf16[384,256]{1,0:T(8,128)(2,1)}, u32[]{:S(2)}, u32[]{:S(2)}) %collective-permute-start) | collective-permute-done | bytes 196640 | tf_op jit(solution)/shard_map/while/body/eval_jaxpr/ppermute | solution.py:16
  100.7 8.3 %collective-permute-done = bf16[384,256]{1,0:T(8,128)(2,1)} collective-permute-done((bf16[384,256]{1,0:T(8,128)(2,1)S(1)}, bf16[384,256]{1,0:T(8,128)(2,1)}, u32[]{:S(2)}, u32[]{:S(2)}) %collective-permute-start) | collective-permute-done | bytes 196640 | tf_op jit(solution)/shard_map/while/body/eval_jaxpr/ppermute | solution.py:16
  110.5 8.3 %collective-permute-done = bf16[384,256]{1,0:T(8,128)(2,1)} collective-permute-done((bf16[384,256]{1,0:T(8,128)(2,1)S(1)}, bf16[384,256]{1,0:T(8,128)(2,1)}, u32[]{:S(2)}, u32[]{:S(2)}) %collective-permute-start) | collective-permute-done | bytes 196640 | tf_op jit(solution)/shard_map/while/body/eval_jaxpr/ppermute | solution.py:16
  120.2 8.3 %collective-permute-done = bf16[384,256]{1,0:T(8,128)(2,1)} collective-permute-done((bf16[384,256]{1,0:T(8,128)(2,1)S(1)}, bf16[384,256]{1,0:T(8,128)(2,1)}, u32[]{:S(2)}, u32[]{:S(2)}) %collective-permute-start) | collective-permute-done | bytes 196640 | tf_op jit(solution)/shard_map/while/body/eval_jaxpr/ppermute | solution.py:16
  129.9 8.3 %collective-permute-done = bf16[384,256]{1,0:T(8,128)(2,1)} collective-permute-done((bf16[384,256]{1,0:T(8,128)(2,1)S(1)}, bf16[384,256]{1,0:T(8,128)(2,1)}, u32[]{:S(2)}, u32[]{:S(2)}) %collective-permute-start) | collective-permute-done | bytes 196640 | tf_op jit(solution)/shard_map/while/body/eval_jaxpr/ppermute | solution.py:16
  149.4 8.3 %collective-permute-done = bf16[384,256]{1,0:T(8,128)(2,1)} collective-permute-done((bf16[384,256]{1,0:T(8,128)(2,1)S(1)}, bf16[384,256]{1,0:T(8,128)(2,1)}, u32[]{:S(2)}, u32[]{:S(2)}) %collective-permute-start) | collective-permute-done | bytes 196640 | tf_op jit(solution)/shard_map/while/body/eval_jaxpr/ppermute | solution.py:16
  168.3 500.2 %while.48 = (s32[]{:T(128)}, f32[2,192,4,128]{3,1,2,0:T(8,128)}, bf16[384,256]{1,0:T(8,128)(2,1)}, f32[384,256]{1,0:T(8,128)}, s32[]{:T(128)}, /*index=5*/s32[]{...) while((s32[]{:T(128)}, f32[2,192,4,128]{3,1,2,0:T(8,128)}, ...), condition=%wide.region_31.32_spmd.clone, body=%wide.region_22.31_spmd.clone.sunk | while | flops 761021184 | bytes 36630940 | solution.py:211
  210.8 16.0 %collective-permute-done.2 = f32[384,256]{1,0:T(8,128)} collective-permute-done((f32[384,256]{1,0:T(8,128)}, f32[384,256]{1,0:T(8,128)}, u32[]{:S(2)}, u32[]{:S(2)}) %collective-permute-start.2) | collective-permute-done | bytes 393248 | tf_op jit(solution)/shard_map/while/body/eval_jaxpr/ppermute | solution.py:16
  240.2 17.9 %collective-permute-done.2 = f32[384,256]{1,0:T(8,128)} collective-permute-done((f32[384,256]{1,0:T(8,128)}, f32[384,256]{1,0:T(8,128)}, u32[]{:S(2)}, u32[]{:S(2)}) %collective-permute-start.2) | collective-permute-done | bytes 393248 | tf_op jit(solution)/shard_map/while/body/eval_jaxpr/ppermute | solution.py:16
  271.4 17.9 %collective-permute-done.2 = f32[384,256]{1,0:T(8,128)} collective-permute-done((f32[384,256]{1,0:T(8,128)}, f32[384,256]{1,0:T(8,128)}, u32[]{:S(2)}, u32[]{:S(2)}) %collective-permute-start.2) | collective-permute-done | bytes 393248 | tf_op jit(solution)/shard_map/while/body/eval_jaxpr/ppermute | solution.py:16
  302.6 17.9 %collective-permute-done.2 = f32[384,256]{1,0:T(8,128)} collective-permute-done((f32[384,256]{1,0:T(8,128)}, f32[384,256]{1,0:T(8,128)}, u32[]{:S(2)}, u32[]{:S(2)}) %collective-permute-start.2) | collective-permute-done | bytes 393248 | tf_op jit(solution)/shard_map/while/body/eval_jaxpr/ppermute | solution.py:16
  333.8 17.9 %collective-permute-done.2 = f32[384,256]{1,0:T(8,128)} collective-permute-done((f32[384,256]{1,0:T(8,128)}, f32[384,256]{1,0:T(8,128)}, u32[]{:S(2)}, u32[]{:S(2)}) %collective-permute-start.2) | collective-permute-done | bytes 393248 | tf_op jit(solution)/shard_map/while/body/eval_jaxpr/ppermute | solution.py:16
  365.0 17.9 %collective-permute-done.2 = f32[384,256]{1,0:T(8,128)} collective-permute-done((f32[384,256]{1,0:T(8,128)}, f32[384,256]{1,0:T(8,128)}, u32[]{:S(2)}, u32[]{:S(2)}) %collective-permute-start.2) | collective-permute-done | bytes 393248 | tf_op jit(solution)/shard_map/while/body/eval_jaxpr/ppermute | solution.py:16
  396.2 17.9 %collective-permute-done.2 = f32[384,256]{1,0:T(8,128)} collective-permute-done((f32[384,256]{1,0:T(8,128)}, f32[384,256]{1,0:T(8,128)}, u32[]{:S(2)}, u32[]{:S(2)}) %collective-permute-start.2) | collective-permute-done | bytes 393248 | tf_op jit(solution)/shard_map/while/body/eval_jaxpr/ppermute | solution.py:16
  427.4 17.9 %collective-permute-done.2 = f32[384,256]{1,0:T(8,128)} collective-permute-done((f32[384,256]{1,0:T(8,128)}, f32[384,256]{1,0:T(8,128)}, u32[]{:S(2)}, u32[]{:S(2)}) %collective-permute-start.2) | collective-permute-done | bytes 393248 | tf_op jit(solution)/shard_map/while/body/eval_jaxpr/ppermute | solution.py:16
  458.6 17.9 %collective-permute-done.2 = f32[384,256]{1,0:T(8,128)} collective-permute-done((f32[384,256]{1,0:T(8,128)}, f32[384,256]{1,0:T(8,128)}, u32[]{:S(2)}, u32[]{:S(2)}) %collective-permute-start.2) | collective-permute-done | bytes 393248 | tf_op jit(solution)/shard_map/while/body/eval_jaxpr/ppermute | solution.py:16
  489.8 17.9 %collective-permute-done.2 = f32[384,256]{1,0:T(8,128)} collective-permute-done((f32[384,256]{1,0:T(8,128)}, f32[384,256]{1,0:T(8,128)}, u32[]{:S(2)}, u32[]{:S(2)}) %collective-permute-start.2) | collective-permute-done | bytes 393248 | tf_op jit(solution)/shard_map/while/body/eval_jaxpr/ppermute | solution.py:16
  521.1 17.9 %collective-permute-done.2 = f32[384,256]{1,0:T(8,128)} collective-permute-done((f32[384,256]{1,0:T(8,128)}, f32[384,256]{1,0:T(8,128)}, u32[]{:S(2)}, u32[]{:S(2)}) %collective-permute-start.2) | collective-permute-done | bytes 393248 | tf_op jit(solution)/shard_map/while/body/eval_jaxpr/ppermute | solution.py:16
  552.3 17.9 %collective-permute-done.2 = f32[384,256]{1,0:T(8,128)} collective-permute-done((f32[384,256]{1,0:T(8,128)}, f32[384,256]{1,0:T(8,128)}, u32[]{:S(2)}, u32[]{:S(2)}) %collective-permute-start.2) | collective-permute-done | bytes 393248 | tf_op jit(solution)/shard_map/while/body/eval_jaxpr/ppermute | solution.py:16
  583.5 17.9 %collective-permute-done.2 = f32[384,256]{1,0:T(8,128)} collective-permute-done((f32[384,256]{1,0:T(8,128)}, f32[384,256]{1,0:T(8,128)}, u32[]{:S(2)}, u32[]{:S(2)}) %collective-permute-start.2) | collective-permute-done | bytes 393248 | tf_op jit(solution)/shard_map/while/body/eval_jaxpr/ppermute | solution.py:16
  614.7 17.9 %collective-permute-done.2 = f32[384,256]{1,0:T(8,128)} collective-permute-done((f32[384,256]{1,0:T(8,128)}, f32[384,256]{1,0:T(8,128)}, u32[]{:S(2)}, u32[]{:S(2)}) %collective-permute-start.2) | collective-permute-done | bytes 393248 | tf_op jit(solution)/shard_map/while/body/eval_jaxpr/ppermute | solution.py:16
  645.9 22.6 %collective-permute-done.2 = f32[384,256]{1,0:T(8,128)} collective-permute-done((f32[384,256]{1,0:T(8,128)}, f32[384,256]{1,0:T(8,128)}, u32[]{:S(2)}, u32[]{:S(2)}) %collective-permute-start.2) | collective-permute-done | bytes 393248 | tf_op jit(solution)/shard_map/while/body/eval_jaxpr/ppermute | solution.py:16
  710.7 40.5 %reduce-scatter.5.cloned.1.call-done = f32[48,256]{1,0:T(8,128)} async-done(((f32[384,256]{1,0:T(8,128)}), f32[48,256]{1,0:T(8,128)}) %reduce-scatter.5.cloned.1.call-update) | async-done | bytes 49168 | tf_op jit(solution)/shard_map/reduce_scatter | solution.py:227
  763.5 10.2 %fusion.122 = (bf16[128,1536]{1,0:T(8,128)(2,1)}, bf16[128,1536]{1,0:T(8,128)(2,1)}) fusion(bf16[128,1536]{1,0:T(8,128)(2,1)S(1)} %copy-done.11, bf16[128,1536]{1,0:T(8,128)(2,1)S(1)} %copy-done.10, bf16[128,4096]{1,0:T(8,128)(2,1)} %bitcast.52, bf16[1,1536,4096]{2,1,0:T(8,128)(2,1)} %param.39, f32[128]{0:T(128)S(1)} %reshape.218), kind=kOutput, calls=%fused_computation.204 | convolution fusion | flops 1613758464 | bytes 15204864 | tf_op jit(solution)/shard_map/dot_general | solution.py:268
  (931 shorter events, 352.9 us)
Async XLA Ops:
  7.2 702.2 %reduce-scatter.3.cloned.1.call-start = ((), (), s32[]{:S(2)}) async-start(), calls=%async_computation.5 | async-start | bytes 442368 | tf_op jit(solution)/shard_map/reduce_scatter | solution.py:226
  170.0 17.6 %collective-permute-start.1 = (bf16[384,256]{1,0:T(8,128)(2,1)}, bf16[384,256]{1,0:T(8,128)(2,1)}, u32[]{:S(2)}, u32[]{:S(2)}) collective-permute-start(bf16[384,256]{1,0:T(8,128)(2,1)} %copy.132), channel_id=1, source_target_pairs={{120,0},{0,8},{8,16},{16,24},{24,32},{32,40},{40,48},{48,56},{56,6... | collective-permute-start | bytes 589832 | tf_op jit(solution)/shard_map/while/body/eval_jaxpr/ppermute | solution.py:16
  197.2 13.6 %collective-permute-start.1 = (bf16[384,256]{1,0:T(8,128)(2,1)}, bf16[384,256]{1,0:T(8,128)(2,1)}, u32[]{:S(2)}, u32[]{:S(2)}) collective-permute-start(bf16[384,256]{1,0:T(8,128)(2,1)} %copy.132), channel_id=1, source_target_pairs={{120,0},{0,8},{8,16},{16,24},{24,32},{32,40},{40,48},{48,56},{56,6... | collective-permute-start | bytes 589832 | tf_op jit(solution)/shard_map/while/body/eval_jaxpr/ppermute | solution.py:16
  204.8 22.1 %collective-permute-start.2 = (f32[384,256]{1,0:T(8,128)}, f32[384,256]{1,0:T(8,128)}, u32[]{:S(2)}, u32[]{:S(2)}) collective-permute-start(f32[384,256]{1,0:T(8,128)} %maximum_add_fusion.5), channel_id=1, source_target_pairs={{120,0},{0,8},{8,16},{16,24},{24,32},{32,40},{40,48},{48,56},{56,6... | collective-permute-start | bytes 1179656 | tf_op jit(solution)/shard_map/while/body/eval_jaxpr/ppermute | solution.py:16
  228.4 11.7 %collective-permute-start.1 = (bf16[384,256]{1,0:T(8,128)(2,1)}, bf16[384,256]{1,0:T(8,128)(2,1)}, u32[]{:S(2)}, u32[]{:S(2)}) collective-permute-start(bf16[384,256]{1,0:T(8,128)(2,1)} %copy.132), channel_id=1, source_target_pairs={{120,0},{0,8},{8,16},{16,24},{24,32},{32,40},{40,48},{48,56},{56,6... | collective-permute-start | bytes 589832 | tf_op jit(solution)/shard_map/while/body/eval_jaxpr/ppermute | solution.py:16
  236.0 22.1 %collective-permute-start.2 = (f32[384,256]{1,0:T(8,128)}, f32[384,256]{1,0:T(8,128)}, u32[]{:S(2)}, u32[]{:S(2)}) collective-permute-start(f32[384,256]{1,0:T(8,128)} %maximum_add_fusion.5), channel_id=1, source_target_pairs={{120,0},{0,8},{8,16},{16,24},{24,32},{32,40},{40,48},{48,56},{56,6... | collective-permute-start | bytes 1179656 | tf_op jit(solution)/shard_map/while/body/eval_jaxpr/ppermute | solution.py:16
  267.2 22.1 %collective-permute-start.2 = (f32[384,256]{1,0:T(8,128)}, f32[384,256]{1,0:T(8,128)}, u32[]{:S(2)}, u32[]{:S(2)}) collective-permute-start(f32[384,256]{1,0:T(8,128)} %maximum_add_fusion.5), channel_id=1, source_target_pairs={{120,0},{0,8},{8,16},{16,24},{24,32},{32,40},{40,48},{48,56},{56,6... | collective-permute-start | bytes 1179656 | tf_op jit(solution)/shard_map/while/body/eval_jaxpr/ppermute | solution.py:16
  298.4 22.1 %collective-permute-start.2 = (f32[384,256]{1,0:T(8,128)}, f32[384,256]{1,0:T(8,128)}, u32[]{:S(2)}, u32[]{:S(2)}) collective-permute-start(f32[384,256]{1,0:T(8,128)} %maximum_add_fusion.5), channel_id=1, source_target_pairs={{120,0},{0,8},{8,16},{16,24},{24,32},{32,40},{40,48},{48,56},{56,6... | collective-permute-start | bytes 1179656 | tf_op jit(solution)/shard_map/while/body/eval_jaxpr/ppermute | solution.py:16
  329.6 22.1 %collective-permute-start.2 = (f32[384,256]{1,0:T(8,128)}, f32[384,256]{1,0:T(8,128)}, u32[]{:S(2)}, u32[]{:S(2)}) collective-permute-start(f32[384,256]{1,0:T(8,128)} %maximum_add_fusion.5), channel_id=1, source_target_pairs={{120,0},{0,8},{8,16},{16,24},{24,32},{32,40},{40,48},{48,56},{56,6... | collective-permute-start | bytes 1179656 | tf_op jit(solution)/shard_map/while/body/eval_jaxpr/ppermute | solution.py:16
  353.3 11.7 %collective-permute-start.1 = (bf16[384,256]{1,0:T(8,128)(2,1)}, bf16[384,256]{1,0:T(8,128)(2,1)}, u32[]{:S(2)}, u32[]{:S(2)}) collective-permute-start(bf16[384,256]{1,0:T(8,128)(2,1)} %copy.132), channel_id=1, source_target_pairs={{120,0},{0,8},{8,16},{16,24},{24,32},{32,40},{40,48},{48,56},{56,6... | collective-permute-start | bytes 589832 | tf_op jit(solution)/shard_map/while/body/eval_jaxpr/ppermute | solution.py:16
  360.8 22.1 %collective-permute-start.2 = (f32[384,256]{1,0:T(8,128)}, f32[384,256]{1,0:T(8,128)}, u32[]{:S(2)}, u32[]{:S(2)}) collective-permute-start(f32[384,256]{1,0:T(8,128)} %maximum_add_fusion.5), channel_id=1, source_target_pairs={{120,0},{0,8},{8,16},{16,24},{24,32},{32,40},{40,48},{48,56},{56,6... | collective-permute-start | bytes 1179656 | tf_op jit(solution)/shard_map/while/body/eval_jaxpr/ppermute | solution.py:16
  384.5 11.7 %collective-permute-start.1 = (bf16[384,256]{1,0:T(8,128)(2,1)}, bf16[384,256]{1,0:T(8,128)(2,1)}, u32[]{:S(2)}, u32[]{:S(2)}) collective-permute-start(bf16[384,256]{1,0:T(8,128)(2,1)} %copy.132), channel_id=1, source_target_pairs={{120,0},{0,8},{8,16},{16,24},{24,32},{32,40},{40,48},{48,56},{56,6... | collective-permute-start | bytes 589832 | tf_op jit(solution)/shard_map/while/body/eval_jaxpr/ppermute | solution.py:16
  392.0 22.1 %collective-permute-start.2 = (f32[384,256]{1,0:T(8,128)}, f32[384,256]{1,0:T(8,128)}, u32[]{:S(2)}, u32[]{:S(2)}) collective-permute-start(f32[384,256]{1,0:T(8,128)} %maximum_add_fusion.5), channel_id=1, source_target_pairs={{120,0},{0,8},{8,16},{16,24},{24,32},{32,40},{40,48},{48,56},{56,6... | collective-permute-start | bytes 1179656 | tf_op jit(solution)/shard_map/while/body/eval_jaxpr/ppermute | solution.py:16
  415.7 11.7 %collective-permute-start.1 = (bf16[384,256]{1,0:T(8,128)(2,1)}, bf16[384,256]{1,0:T(8,128)(2,1)}, u32[]{:S(2)}, u32[]{:S(2)}) collective-permute-start(bf16[384,256]{1,0:T(8,128)(2,1)} %copy.132), channel_id=1, source_target_pairs={{120,0},{0,8},{8,16},{16,24},{24,32},{32,40},{40,48},{48,56},{56,6... | collective-permute-start | bytes 589832 | tf_op jit(solution)/shard_map/while/body/eval_jaxpr/ppermute | solution.py:16
  423.2 22.1 %collective-permute-start.2 = (f32[384,256]{1,0:T(8,128)}, f32[384,256]{1,0:T(8,128)}, u32[]{:S(2)}, u32[]{:S(2)}) collective-permute-start(f32[384,256]{1,0:T(8,128)} %maximum_add_fusion.5), channel_id=1, source_target_pairs={{120,0},{0,8},{8,16},{16,24},{24,32},{32,40},{40,48},{48,56},{56,6... | collective-permute-start | bytes 1179656 | tf_op jit(solution)/shard_map/while/body/eval_jaxpr/ppermute | solution.py:16
  446.9 11.7 %collective-permute-start.1 = (bf16[384,256]{1,0:T(8,128)(2,1)}, bf16[384,256]{1,0:T(8,128)(2,1)}, u32[]{:S(2)}, u32[]{:S(2)}) collective-permute-start(bf16[384,256]{1,0:T(8,128)(2,1)} %copy.132), channel_id=1, source_target_pairs={{120,0},{0,8},{8,16},{16,24},{24,32},{32,40},{40,48},{48,56},{56,6... | collective-permute-start | bytes 589832 | tf_op jit(solution)/shard_map/while/body/eval_jaxpr/ppermute | solution.py:16
  454.4 22.1 %collective-permute-start.2 = (f32[384,256]{1,0:T(8,128)}, f32[384,256]{1,0:T(8,128)}, u32[]{:S(2)}, u32[]{:S(2)}) collective-permute-start(f32[384,256]{1,0:T(8,128)} %maximum_add_fusion.5), channel_id=1, source_target_pairs={{120,0},{0,8},{8,16},{16,24},{24,32},{32,40},{40,48},{48,56},{56,6... | collective-permute-start | bytes 1179656 | tf_op jit(solution)/shard_map/while/body/eval_jaxpr/ppermute | solution.py:16
  478.1 11.7 %collective-permute-start.1 = (bf16[384,256]{1,0:T(8,128)(2,1)}, bf16[384,256]{1,0:T(8,128)(2,1)}, u32[]{:S(2)}, u32[]{:S(2)}) collective-permute-start(bf16[384,256]{1,0:T(8,128)(2,1)} %copy.132), channel_id=1, source_target_pairs={{120,0},{0,8},{8,16},{16,24},{24,32},{32,40},{40,48},{48,56},{56,6... | collective-permute-start | bytes 589832 | tf_op jit(solution)/shard_map/while/body/eval_jaxpr/ppermute | solution.py:16
  485.6 22.1 %collective-permute-start.2 = (f32[384,256]{1,0:T(8,128)}, f32[384,256]{1,0:T(8,128)}, u32[]{:S(2)}, u32[]{:S(2)}) collective-permute-start(f32[384,256]{1,0:T(8,128)} %maximum_add_fusion.5), channel_id=1, source_target_pairs={{120,0},{0,8},{8,16},{16,24},{24,32},{32,40},{40,48},{48,56},{56,6... | collective-permute-start | bytes 1179656 | tf_op jit(solution)/shard_map/while/body/eval_jaxpr/ppermute | solution.py:16
  509.3 11.7 %collective-permute-start.1 = (bf16[384,256]{1,0:T(8,128)(2,1)}, bf16[384,256]{1,0:T(8,128)(2,1)}, u32[]{:S(2)}, u32[]{:S(2)}) collective-permute-start(bf16[384,256]{1,0:T(8,128)(2,1)} %copy.132), channel_id=1, source_target_pairs={{120,0},{0,8},{8,16},{16,24},{24,32},{32,40},{40,48},{48,56},{56,6... | collective-permute-start | bytes 589832 | tf_op jit(solution)/shard_map/while/body/eval_jaxpr/ppermute | solution.py:16
  516.8 22.1 %collective-permute-start.2 = (f32[384,256]{1,0:T(8,128)}, f32[384,256]{1,0:T(8,128)}, u32[]{:S(2)}, u32[]{:S(2)}) collective-permute-start(f32[384,256]{1,0:T(8,128)} %maximum_add_fusion.5), channel_id=1, source_target_pairs={{120,0},{0,8},{8,16},{16,24},{24,32},{32,40},{40,48},{48,56},{56,6... | collective-permute-start | bytes 1179656 | tf_op jit(solution)/shard_map/while/body/eval_jaxpr/ppermute | solution.py:16
  540.5 11.7 %collective-permute-start.1 = (bf16[384,256]{1,0:T(8,128)(2,1)}, bf16[384,256]{1,0:T(8,128)(2,1)}, u32[]{:S(2)}, u32[]{:S(2)}) collective-permute-start(bf16[384,256]{1,0:T(8,128)(2,1)} %copy.132), channel_id=1, source_target_pairs={{120,0},{0,8},{8,16},{16,24},{24,32},{32,40},{40,48},{48,56},{56,6... | collective-permute-start | bytes 589832 | tf_op jit(solution)/shard_map/while/body/eval_jaxpr/ppermute | solution.py:16
  548.0 22.1 %collective-permute-start.2 = (f32[384,256]{1,0:T(8,128)}, f32[384,256]{1,0:T(8,128)}, u32[]{:S(2)}, u32[]{:S(2)}) collective-permute-start(f32[384,256]{1,0:T(8,128)} %maximum_add_fusion.5), channel_id=1, source_target_pairs={{120,0},{0,8},{8,16},{16,24},{24,32},{32,40},{40,48},{48,56},{56,6... | collective-permute-start | bytes 1179656 | tf_op jit(solution)/shard_map/while/body/eval_jaxpr/ppermute | solution.py:16
  571.7 11.7 %collective-permute-start.1 = (bf16[384,256]{1,0:T(8,128)(2,1)}, bf16[384,256]{1,0:T(8,128)(2,1)}, u32[]{:S(2)}, u32[]{:S(2)}) collective-permute-start(bf16[384,256]{1,0:T(8,128)(2,1)} %copy.132), channel_id=1, source_target_pairs={{120,0},{0,8},{8,16},{16,24},{24,32},{32,40},{40,48},{48,56},{56,6... | collective-permute-start | bytes 589832 | tf_op jit(solution)/shard_map/while/body/eval_jaxpr/ppermute | solution.py:16
  579.3 22.1 %collective-permute-start.2 = (f32[384,256]{1,0:T(8,128)}, f32[384,256]{1,0:T(8,128)}, u32[]{:S(2)}, u32[]{:S(2)}) collective-permute-start(f32[384,256]{1,0:T(8,128)} %maximum_add_fusion.5), channel_id=1, source_target_pairs={{120,0},{0,8},{8,16},{16,24},{24,32},{32,40},{40,48},{48,56},{56,6... | collective-permute-start | bytes 1179656 | tf_op jit(solution)/shard_map/while/body/eval_jaxpr/ppermute | solution.py:16
  602.9 11.7 %collective-permute-start.1 = (bf16[384,256]{1,0:T(8,128)(2,1)}, bf16[384,256]{1,0:T(8,128)(2,1)}, u32[]{:S(2)}, u32[]{:S(2)}) collective-permute-start(bf16[384,256]{1,0:T(8,128)(2,1)} %copy.132), channel_id=1, source_target_pairs={{120,0},{0,8},{8,16},{16,24},{24,32},{32,40},{40,48},{48,56},{56,6... | collective-permute-start | bytes 589832 | tf_op jit(solution)/shard_map/while/body/eval_jaxpr/ppermute | solution.py:16
  610.5 22.1 %collective-permute-start.2 = (f32[384,256]{1,0:T(8,128)}, f32[384,256]{1,0:T(8,128)}, u32[]{:S(2)}, u32[]{:S(2)}) collective-permute-start(f32[384,256]{1,0:T(8,128)} %maximum_add_fusion.5), channel_id=1, source_target_pairs={{120,0},{0,8},{8,16},{16,24},{24,32},{32,40},{40,48},{48,56},{56,6... | collective-permute-start | bytes 1179656 | tf_op jit(solution)/shard_map/while/body/eval_jaxpr/ppermute | solution.py:16
  634.1 11.7 %collective-permute-start.1 = (bf16[384,256]{1,0:T(8,128)(2,1)}, bf16[384,256]{1,0:T(8,128)(2,1)}, u32[]{:S(2)}, u32[]{:S(2)}) collective-permute-start(bf16[384,256]{1,0:T(8,128)(2,1)} %copy.132), channel_id=1, source_target_pairs={{120,0},{0,8},{8,16},{16,24},{24,32},{32,40},{40,48},{48,56},{56,6... | collective-permute-start | bytes 589832 | tf_op jit(solution)/shard_map/while/body/eval_jaxpr/ppermute | solution.py:16
  641.7 26.8 %collective-permute-start.2 = (f32[384,256]{1,0:T(8,128)}, f32[384,256]{1,0:T(8,128)}, u32[]{:S(2)}, u32[]{:S(2)}) collective-permute-start(f32[384,256]{1,0:T(8,128)} %maximum_add_fusion.5), channel_id=1, source_target_pairs={{120,0},{0,8},{8,16},{16,24},{24,32},{32,40},{40,48},{48,56},{56,6... | collective-permute-start | bytes 1179656 | tf_op jit(solution)/shard_map/while/body/eval_jaxpr/ppermute | solution.py:16
  696.2 56.5 %all-to-all-start = ((bf16[8,16,4096]{2,1,0:T(8,128)(2,1)}), bf16[8,16,4096]{2,1,0:T(8,128)(2,1)}, u32[]{:S(2)}, u32[]{:S(2)}) async-start(bf16[8,16,4096]{2,1,0:T(8,128)(2,1)} %broadcast_select_fusion), calls=%async_computation.2 | async-start | bytes 2097152 | tf_op jit(solution)/shard_map/all_to_all | solution.py:252
  700.4 50.8 %reduce-scatter.5.cloned.1.call-start = ((), (), s32[]{:S(2)}) async-start(), calls=%async_computation.6 | async-start | bytes 442368 | tf_op jit(solution)/shard_map/reduce_scatter | solution.py:227
  760.2 13.6 %all-to-all-start.1 = ((f32[8,1,16]{2,1,0:T(1,128)}), f32[8,1,16]{2,1,0:T(1,128)S(1)}, u32[]{:S(2)}, u32[]{:S(2)}) async-start(f32[8,1,16]{2,1,0:T(1,128)} %bitcast.54), calls=%async_computation.3 | async-start | bytes 8192 | tf_op jit(solution)/shard_map/all_to_all | solution.py:276
  (93 other events, 2128.1 us)
Sparse Core Ops, SparseCore 0:
  670.4 38.8 reduce-scatter.2
  712.4 38.7 reduce-scatter.4
where the time goes:
time: 800 us; the launch traced here: 789 us
  waiting for transfers between devices  460 us (58%)
  other arithmetic  139 us (17%)
  local copies, waits for them, and re-layouts  129 us (16%)
  matrix products  25.8 us (3%)
  starting transfers between devices  14.8 us (2%)
  between operations  14.4 us (2%)
    ppermute x48, waiting for transfers between devices, passed_along(): return lax.ppermute(block, axis, route)  410 us
    while x144, local copies, waits for them, and re-layouts  49.2 us
    reduce_scatter x1, waiting for transfers between devices, shards(): lax.psum_scatter(value_full, 'exp', scatter_dimension=0, tiled=True)  40.5 us
    another operation x32, other arithmetic, block_grads(): return (jnp.stack(query_terms), jnp.concatenate(pair_terms, axis=0))  33.2 us
    add x16, other arithmetic, grad_step(): query_acc + query_term  32.9 us
    add x32, other arithmetic, block_grads(): pair_terms[key_side] = pair_terms[key_side] + pair_piece  32.9 us
    add x16, other arithmetic, grad_step(): pair_acc + pair_term  28.7 us
    slice x16, local copies, waits for them, and re-layouts, block_grads(): kv_half = kv_block[key_side * half_rows:(key_side + 1) * half_rows]  25.5 us
  transfers between devices with their start and end apart: 53, of which 35 were waited for; matrix products, arithmetic and copies ran while one was open for 26% of the time, Pallas kernels for 0%

commit v1 on v0

v1 whole, which is shorter than its diff:
```python
import functools

import jax
import jax.numpy as jnp
from jax import lax
from jax.experimental import pallas as pl
from jax.experimental.pallas import tpu as pltpu
from jax.sharding import PartitionSpec as P

QHEADS = 32
KVHEADS = 2
HEAD = 128
TOPK = 8
CAP = 16
LOG2E = 1.4426950408889634
SCALE = HEAD ** (-0.5)
MESH = pl.DeviceIdType.MESH
NT = (((1,), (1,)), ((), ()))
TN = (((0,), (0,)), ((), ()))
NN = (((1,), (0,)), ((), ()))


def dot(a, b, dims):
    return lax.dot_general(a, b, dims, preferred_element_type=jnp.float32)


def body(
    q_ref,
    k_ref,
    v_ref,
    do_ref,
    moe_ref,
    ids_ref,
    gw_ref,
    sg_ref,
    su_ref,
    w_ref,
    dq_ref,
    dk_ref,
    dv_ref,
    gg_ref,
    gp_ref,
    up_ref,
    kv,
    qd_own,
    qd_send,
    qd_for,
    probs,
    dprob,
    maxes,
    dq_acc,
    dkv,
    dq_send,
    dq_recv,
    merge_recv,
    ea_recv,
    total,
    eb_recv,
    send_rows,
    recv_rows,
    onehot,
    score_send,
    score_recv,
    w_buf,
    w_sem,
    a_sem,
    b_sem,
    relay_sem,
    c_sem,
    d_sem,
    merge_sem,
    ea_sem,
    eb_sem,
    score_sem,
):
    c = lax.axis_index("ctx")
    e = lax.axis_index("exp")
    rows = q_ref.shape[0]
    sub = rows // 2
    heads = q_ref.shape[1] // HEAD
    width = heads * sub
    tokens, model = moe_ref.shape
    hidden = sg_ref.shape[1]
    slots = sg_ref.shape[0]
    z_hi, x, core = c // 8, (c // 2) % 4, c % 2
    chip = c // 2
    y, z_lo = e // 2, e % 2
    kv_head = e // 4

    def ctx_peer(turn, shift):
        far_z = 1 - z_hi if turn else z_hi
        far_zl = 1 - z_lo if turn else z_lo
        far_chip = far_z * 4 + (x + shift) % 4
        return far_chip, (far_chip * 2 + core, y * 2 + far_zl)

    relations = [(0, 1), (0, 3), (1, 0), (0, 2), (1, 1), (1, 3), (1, 2)]
    other_core = (c + 1 - 2 * core, e)
    partner = (15 - c, y * 2 + 1 - z_lo)

    def remote(src, dst, sems, index, device):
        return pltpu.make_async_remote_copy(
            src_ref=src,
            dst_ref=dst,
            send_sem=sems.at[0, index],
            recv_sem=sems.at[1, index],
            device_id=device,
            device_id_type=MESH,
        )

    chunk = w_buf.shape[1]
    chunks = hidden // chunk

    def weight_copy(i, slot):
        return pltpu.make_async_copy(
            w_ref.at[0, pl.ds(pl.multiple_of(i * chunk, chunk), chunk), :],
            w_buf.at[slot],
            w_sem.at[slot],
        )

    weight_copy(0, 0).start()
    weight_copy(1, 1).start()

    barrier = pltpu.get_barrier_semaphore()
    peers = [ctx_peer(turn, shift)[1] for turn, shift in relations]
    peers += [(c, (e + step) % 8) for step in range(1, 8)]
    peers += [other_core, partner]
    for peer in peers:
        pl.semaphore_signal(barrier, inc=1, device_id=peer, device_id_type=MESH)

    head_cols = pl.ds(pl.multiple_of(kv_head * HEAD, HEAD), HEAD)
    kv[core, chip, :, 0:HEAD] = k_ref[:, head_cols]
    kv[core, chip, :, HEAD : 2 * HEAD] = v_ref[:, head_cols]
    for h in range(heads):
        cols = slice(h * HEAD, (h + 1) * HEAD)
        rows_h = slice(h * sub, (h + 1) * sub)
        qd_own[rows_h, 0:HEAD] = q_ref[0:sub, cols]
        qd_own[rows_h, HEAD : 2 * HEAD] = do_ref[0:sub, cols]
        qd_send[rows_h, 0:HEAD] = q_ref[sub : 2 * sub, cols]
        qd_send[rows_h, HEAD : 2 * HEAD] = do_ref[sub : 2 * sub, cols]

    pl.semaphore_wait(barrier, len(peers))

    own_block = kv.at[core, chip]
    b_copies = []
    for n, (turn, shift) in enumerate(relations):
        copy = remote(own_block, own_block, b_sem, n, ctx_peer(turn, shift)[1])
        copy.start()
        b_copies.append(copy)
    relays = [remote(own_block, own_block, relay_sem, 7, other_core)]
    relays[0].start()
    c_copy = remote(qd_send, qd_for, c_sem, 0, partner)
    c_copy.start()

    lane = lax.broadcasted_iota(jnp.int32, (tokens, slots), 1)
    slot_expert = lane // CAP
    ids = ids_ref[...]
    weights = gw_ref[...].astype(jnp.float32)
    match = jnp.zeros((tokens, slots), jnp.float32)
    weight_of = jnp.zeros((tokens, slots), jnp.float32)
    for k in range(TOPK):
        hit = ids[:, k : k + 1] == slot_expert
        match = jnp.where(hit, 1.0, match)
        weight_of = jnp.where(hit, weights[:, k : k + 1], weight_of)
    row = lax.broadcasted_iota(jnp.int32, (tokens, tokens), 0)
    col = lax.broadcasted_iota(jnp.int32, (tokens, tokens), 1)
    lower = jnp.where(col < row, 1.0, 0.0).astype(jnp.bfloat16)
    rank = dot(lower, match.astype(jnp.bfloat16), NN)
    place = jnp.where(rank == (lane % CAP).astype(jnp.float32), match, 0.0)
    onehot[...] = place
    place_b = place.astype(jnp.bfloat16)
    step_cols = 512

    def gather_cols(i, carry):
        cols = pl.ds(pl.multiple_of(i * step_cols, step_cols), step_cols)
        send_rows[:, cols] = dot(place_b, moe_ref[:, cols], TN).astype(jnp.bfloat16)
        return carry

    lax.fori_loop(0, model // step_cols, gather_cols, 0)
    slot_weight = dot(
        (place * weight_of).astype(jnp.bfloat16), jnp.ones((tokens, HEAD), jnp.bfloat16), TN
    )
    send_rows[:, model : model + HEAD] = slot_weight.astype(jnp.bfloat16)
    own_rows = pl.ds(pl.multiple_of(e * CAP, CAP), CAP)
    a_copies = []
    for step in range(1, 8):
        far = (e + step) % 8
        copy = remote(
            send_rows.at[pl.ds(pl.multiple_of(far * CAP, CAP), CAP), :],
            recv_rows.at[own_rows, :],
            a_sem,
            step - 1,
            (c, far),
        )
        copy.start()
        a_copies.append(copy)
    recv_rows[own_rows, :] = send_rows[own_rows, :]

    dkv[...] = jnp.zeros_like(dkv)

    for n, (turn, shift) in enumerate(relations):
        b_copies[n].wait()
        from_chip = ctx_peer(turn, 4 - shift)[0]
        block = kv.at[core, from_chip]
        relay = remote(block, block, relay_sem, n, other_core)
        relay.start()
        relays.append(relay)
    for relay in relays:
        relay.wait()

    def attend(qd, sub_index, base):
        last = sub_index // 2
        q = qd[:, 0:HEAD]
        do = qd[:, HEAD : 2 * HEAD]

        def first(j, stats, masked):
            m, l, d = stats
            s = dot(kv[j % 2, j // 2, :, 0:HEAD], q, NT) * (SCALE * LOG2E)
            dp = dot(kv[j % 2, j // 2, :, HEAD : 2 * HEAD], do, NT)
            if masked:
                key_at = lax.broadcasted_iota(jnp.int32, (rows, width), 0) + j * rows
                query_at = (
                    lax.broadcasted_iota(jnp.int32, (rows, width), 1) % sub + sub_index * sub
                )
                s = jnp.where(key_at <= query_at, s, -jnp.inf)
            new = jnp.maximum(m, jnp.max(s, axis=0, keepdims=True))
            factor = jnp.exp2(m - new)
            ex = jnp.exp2(s - new)
            l = l * factor + jnp.sum(ex, axis=0, keepdims=True)
            d = d * factor + jnp.sum(ex * dp, axis=0, keepdims=True)
            probs[base + j] = ex.astype(probs.dtype)
            dprob[base + j] = dp
            maxes[base + j] = jnp.broadcast_to(new, (8, width))
            return (new, l, d)

        zero = jnp.zeros((1, width), jnp.float32)
        stats = lax.fori_loop(
            0, last, lambda j, s: first(j, s, False), (jnp.full((1, width), -1e30), zero, zero)
        )
        m, l, d = first(last, stats, True)
        inverse = 1.0 / l
        delta = d * inverse
        dq_acc[...] = jnp.zeros_like(dq_acc)

        def second(j, carry):
            scale = jnp.exp2(maxes[base + j][0:1] - m) * inverse
            p = probs[base + j].astype(jnp.float32) * scale
            ds = p * (dprob[base + j] - delta)
            p_b = p.astype(jnp.bfloat16)
            ds_b = ds.astype(jnp.bfloat16)
            dkv[j % 2, j // 2, :, 0:HEAD] += dot(ds_b, q, NN)
            dkv[j % 2, j // 2, :, HEAD : 2 * HEAD] += dot(p_b, do, NN)
            dq_acc[...] += dot(kv[j % 2, j // 2, :, 0:HEAD], ds_b, TN)
            return carry

        lax.fori_loop(0, last + 1, second, 0)
        return (dq_acc[...] * SCALE).T.astype(jnp.bfloat16)

    dq_own = attend(qd_own, 2 * c, 0)
    for h in range(heads):
        dq_ref[0:sub, h * HEAD : (h + 1) * HEAD] = dq_own[h * sub : (h + 1) * sub]
    c_copy.wait()
    dq_send[...] = attend(qd_for, 31 - 2 * c, 0)
    d_copy = remote(dq_send, dq_recv, d_sem, 0, partner)
    d_copy.start()

    far_core = 1 - core
    kv[far_core] = dkv[far_core].astype(jnp.bfloat16)
    merge_copy = remote(kv.at[far_core], merge_recv, merge_sem, 0, other_core)
    merge_copy.start()
    merge_copy.wait()
    ea_copies = []
    for n, (turn, shift) in enumerate(relations):
        far_chip, device = ctx_peer(turn, shift)
        kv[core, far_chip] = (
            dkv[core, far_chip] + merge_recv[far_chip].astype(jnp.float32)
        ).astype(jnp.bfloat16)
        copy = remote(kv.at[core, far_chip], ea_recv.at[n], ea_sem, n, device)
        copy.start()
        ea_copies.append(copy)
    total[...] = dkv[core, chip] + merge_recv[chip].astype(jnp.float32)

    for copy in a_copies:
        copy.wait()
    weight_col = recv_rows[:, model : model + HEAD].astype(jnp.float32)
    weight_wide = jnp.concatenate([weight_col] * (chunk // HEAD), axis=1)

    def expert_step(i, score):
        slot = i % 2
        weight_copy(i, slot).wait()
        cols = pl.ds(pl.multiple_of(i * chunk, chunk), chunk)
        back = dot(recv_rows[:, 0:model], w_buf[slot], NT)

        @pl.when(i + 2 < chunks)
        def _():
            weight_copy(i + 2, slot).start()

        g = sg_ref[:, cols].astype(jnp.float32)
        u = su_ref[:, cols].astype(jnp.float32)
        sig = 1.0 / (1.0 + jnp.exp(-g))
        silu = g * sig
        act = (silu * u).astype(jnp.bfloat16).astype(jnp.float32)
        act_grad = weight_wide * back
        gp_ref[:, cols] = (act_grad * u * sig * (1.0 + g * (1.0 - sig))).astype(jnp.bfloat16)
        up_ref[:, cols] = (act_grad * silu).astype(jnp.bfloat16)
        return score + jnp.sum(act * back, axis=1, keepdims=True)

    score = lax.fori_loop(0, chunks, expert_step, jnp.zeros((slots, 1), jnp.float32))
    score_send[...] = jnp.broadcast_to(score, (slots, HEAD))
    score_copies = []
    for step in range(1, 8):
        far = (e + step) % 8
        copy = remote(
            score_send.at[pl.ds(pl.multiple_of(far * CAP, CAP), CAP), :],
            score_recv.at[own_rows, :],
            score_sem,
            step - 1,
            (c, far),
        )
        copy.start()
        score_copies.append(copy)
    score_recv[own_rows, :] = score_send[own_rows, :]

    for n in range(7):
        ea_copies[n].wait()
        total[...] += ea_recv[n].astype(jnp.float32)
    part = rows // 8
    eb_copies = []
    for step in range(1, 8):
        far = (e + step) % 8
        copy = remote(
            total.at[pl.ds(pl.multiple_of(far * part, part), part), :],
            eb_recv.at[e],
            eb_sem,
            step - 1,
            (c, far),
        )
        copy.start()
        eb_copies.append(copy)
    eb_recv[e] = total[pl.ds(pl.multiple_of(e * part, part), part), :]

    for copy in score_copies:
        copy.wait()
    score_row = score_recv[...].T[0:1, :]
    picked = onehot[...] * score_row
    out_lane = lax.broadcasted_iota(jnp.int32, (tokens, TOPK), 1)
    gate = jnp.zeros((tokens, TOPK), jnp.float32)
    for k in range(TOPK):
        value = jnp.sum(
            jnp.where(ids[:, k : k + 1] == slot_expert, picked, 0.0), axis=1, keepdims=True
        )
        gate = jnp.where(out_lane == k, value, gate)
    gg_ref[...] = gate

    d_copy.wait()
    for h in range(heads):
        dq_ref[sub : 2 * sub, h * HEAD : (h + 1) * HEAD] = dq_recv[h * sub : (h + 1) * sub]

    for copy in eb_copies:
        copy.wait()
    for kv_index in range(KVHEADS):
        sums = eb_recv[4 * kv_index]
        for n in range(1, 4):
            sums = sums + eb_recv[4 * kv_index + n]
        cols = slice(kv_index * HEAD, (kv_index + 1) * HEAD)
        dk_ref[:, cols] = (sums[:, 0:HEAD] * SCALE).astype(jnp.bfloat16)
        dv_ref[:, cols] = sums[:, HEAD : 2 * HEAD].astype(jnp.bfloat16)


def shards(*arrays):
    queries, keys, _, _, moe_grad, expert_ids, _, saved_gate, _, _ = arrays
    rows, columns = queries.shape
    sub = rows // 2
    width = columns // HEAD * sub
    tokens, model = moe_grad.shape
    slots, hidden = saved_gate.shape
    bf16, f32 = jnp.bfloat16, jnp.float32
    vmem = pl.BlockSpec(memory_space=pltpu.VMEM)
    dma = pltpu.SemaphoreType.DMA
    return pl.pallas_call(
        body,
        out_shape=(
            jax.ShapeDtypeStruct((rows, columns), bf16),
            jax.ShapeDtypeStruct((rows // 8, 2 * HEAD), bf16),
            jax.ShapeDtypeStruct((rows // 8, 2 * HEAD), bf16),
            jax.ShapeDtypeStruct((tokens, TOPK), f32),
            jax.ShapeDtypeStruct((slots, hidden), bf16),
            jax.ShapeDtypeStruct((slots, hidden), bf16),
        ),
        in_specs=[vmem] * 9 + [pl.BlockSpec(memory_space=pl.ANY)],
        out_specs=(vmem,) * 6,
        scratch_shapes=[
            pltpu.VMEM((2, 8, rows, 2 * HEAD), bf16),
            pltpu.VMEM((width, 2 * HEAD), bf16),
            pltpu.VMEM((width, 2 * HEAD), bf16),
            pltpu.VMEM((width, 2 * HEAD), bf16),
            pltpu.VMEM((16, rows, width), bf16),
            pltpu.VMEM((16, rows, width), f32),
            pltpu.VMEM((16, 8, width), f32),
            pltpu.VMEM((HEAD, width), f32),
            pltpu.VMEM((2, 8, rows, 2 * HEAD), f32),
            pltpu.VMEM((width, HEAD), bf16),
            pltpu.VMEM((width, HEAD), bf16),
            pltpu.VMEM((8, rows, 2 * HEAD), bf16),
            pltpu.VMEM((7, rows, 2 * HEAD), bf16),
            pltpu.VMEM((rows, 2 * HEAD), f32),
            pltpu.VMEM((8, rows // 8, 2 * HEAD), f32),
            pltpu.VMEM((slots, model + HEAD), bf16),
            pltpu.VMEM((slots, model + HEAD), bf16),
            pltpu.VMEM((tokens, slots), f32),
            pltpu.VMEM((slots, HEAD), f32),
            pltpu.VMEM((slots, HEAD), f32),
            pltpu.VMEM((2, 256, model), bf16),
            dma((2,)),
            dma((2, 7)),
            dma((2, 7)),
            dma((2, 8)),
            dma((2, 1)),
            dma((2, 1)),
            dma((2, 1)),
            dma((2, 7)),
            dma((2, 7)),
            dma((2, 7)),
        ],
        compiler_params=pltpu.CompilerParams(
            collective_id=0, has_side_effects=True, vmem_limit_bytes=60 * 1024 * 1024
        ),
    )(*arrays)


def solution(mesh):
    both = ("ctx", "exp")
    in_specs = (
        P("ctx", "exp"),
        P("ctx", None),
        P("ctx", None),
        P("ctx", "exp"),
        P(both, None),
        P(both, None),
        P(both, None),
        P(both, None),
        P(both, None),
        P("exp", None, None),
    )
    out_specs = (
        P("ctx", "exp"),
        P(both, None),
        P(both, None),
        P(both, None),
        P(both, None),
        P(both, None),
    )
    return jax.shard_map(shards, mesh=mesh, in_specs=in_specs, out_specs=out_specs, check_vma=False)
```

time: 800 us -> 106 us (0.13); the launches traced: 789 us -> 104 us
  waiting for transfers between devices: 460 us -> 0 us
  other arithmetic: 139 us -> 0 us
  local copies, waits for them, and re-layouts: 129 us -> 12.3 us
  Pallas kernels: 0 us -> 91.6 us
  matrix products: 25.8 us -> 0 us
  starting transfers between devices: 14.8 us -> 0 us
  between operations: 14.4 us -> 0.64 us
    ppermute x48 -> x0, waiting for transfers between devices: 410 us -> none  [passed_along(): return lax.ppermute(block, axis, route)]
    add x163 -> x0, other arithmetic: 95.1 us -> none  [the longest x16 32.9 us: grad_step(): query_acc + query_term]
    pallas_call x0 -> x1, Pallas kernels: none -> 91.6 us  [shards(): pl.pallas_call(body, out_shape=(jax.ShapeDtypeStruct((rows, columns), bf1...]
    while x146 -> x0, local copies, waits for them, and re-layouts: 49.3 us -> none
    reduce_scatter x2 -> x0, waiting for transfers between devices: 46.2 us -> none  [the longest x1 40.5 us: shards(): lax.psum_scatter(value_full, 'exp', scatter_dimension=0, tiled=True)]
    another operation x34 -> x0, other arithmetic: 35.7 us -> none  [the longest x32 33.2 us: block_grads(): return (jnp.stack(query_terms), jnp.concatenate(pair_terms, axis=0))]
    dot_general x23 -> x0, matrix products: 25.8 us -> none  [the longest x1 10.2 us: shards(): lax.dot_general(recv_rows, expert_weight, (((1,), (1,)), ((), ())), prefe...]
    slice x32 -> x0, local copies, waits for them, and re-layouts: 25.7 us -> none  [the longest x16 25.5 us: block_grads(): kv_half = kv_block[key_side * half_rows:(key_side + 1) * half_rows]]
  transfers between devices with their start and end apart: 53 -> 0, of which waited for: 35 -> 0; matrix products, arithmetic and copies ran while one was open for 26% -> 0% of each run, Pallas kernels for 0% -> 0%
where the time goes in v1:
time: 106 us; the launch traced here: 104 us
  Pallas kernels  91.6 us (86%)
  local copies, waits for them, and re-layouts  12.3 us (12%)
    pallas_call x1, Pallas kernels, shards(): pl.pallas_call(body, out_shape=(jax.ShapeDtypeStruct((rows, columns), bf1...  91.6 us
    unnamed x7, local copies, waits for them, and re-layouts  10.8 us

profile of v1, /device:TPU:0, one launch (start us, length us, event | category | flops | bytes accessed | tf_op | source)
XLA Modules:
  0.0 104.5 jit_solution(16038780299651566937)
XLA Ops:
  0.6 1.4 %copy.17.gw_ref = bf16[128,8]{1,0:T(8,128)(2,1)} copy(bf16[128,8]{0,1:T(8,128)(2,1)} %param.16) | data formatting | bytes 4096 | tf_op args[6]
  2.0 1.4 %copy.16.ids_ref = s32[128,8]{1,0:T(8,128)} copy(s32[128,8]{0,1:T(8,128)} %param.15) | data formatting | bytes 8192 | tf_op args[5]
  3.4 91.6 %shard_map.145 = (bf16[384,512]{1,0:T(8,128)(2,1)}, bf16[48,256]{1,0:T(8,128)(2,1)}, bf16[48,256]{1,0:T(8,128)(2,1)}, f32[128,8]{1,0:T(8,128)}, bf16[128,1536]{1,0:T(8,128)(2,1)}, /*index=5*/bf16[128,1536]{1,0:T(8,128)(2,1)}) custom-call(bf16[384,512]{1,0:T(8,128)(2,1)} %q_ref.1, bf16[384,256]{1,0:T(8,128)(2,1)} %k_ref.1, bf16[384,256]{1,0:T(8,128)(2,1)} %v_ref.1, ...), custom_call_target="tpu_custom_call" | custom-call | tf_op jit(solution)/shard_map/pallas_call | solution.py:379
  95.0 1.5 %copy.18 = f32[128,8]{0,1:T(8,128)} copy(f32[128,8]{1,0:T(8,128)} %get-tuple-element.9) | data formatting | bytes 8192 | tf_op jit(solution)/shard_map/pallas_call | solution.py:379
  96.5 1.8 %copy.24 = bf16[384,512]{1,0:T(8,128)(2,1)} copy(bf16[384,512]{1,0:T(8,128)(2,1)} %get-tuple-element.18) | data formatting | bytes 786432
  98.3 1.3 %copy.25 = bf16[48,256]{1,0:T(8,128)(2,1)} copy(bf16[48,256]{1,0:T(8,128)(2,1)} %get-tuple-element.19) | data formatting | bytes 49152
  99.6 1.3 %copy.26 = bf16[48,256]{1,0:T(8,128)(2,1)} copy(bf16[48,256]{1,0:T(8,128)(2,1)} %get-tuple-element.20) | data formatting | bytes 49152
  101.0 1.8 %copy.27 = bf16[128,1536]{1,0:T(8,128)(2,1)} copy(bf16[128,1536]{1,0:T(8,128)(2,1)} %get-tuple-element.22) | data formatting | bytes 786432
  102.7 1.8 %copy.28 = bf16[128,1536]{1,0:T(8,128)(2,1)} copy(bf16[128,1536]{1,0:T(8,128)(2,1)} %get-tuple-element.23) | data formatting | bytes 786432

commit v2 on v1

v2 whole, which is shorter than its diff:
```python
import jax
import jax.numpy as jnp
from jax import lax
from jax.experimental import pallas as pl
from jax.experimental.pallas import tpu as pltpu
from jax.sharding import PartitionSpec as P

KVHEADS = 2
HEAD = 128
TOPK = 8
CAP = 16
LOG2E = 1.4426950408889634
SCALE = HEAD ** (-0.5)
MESH = pl.DeviceIdType.MESH
NT = (((1,), (1,)), ((), ()))
TN = (((0,), (0,)), ((), ()))
NN = (((1,), (0,)), ((), ()))


def dot(a, b, dims):
    return lax.dot_general(a, b, dims, preferred_element_type=jnp.float32)


def flip(a, b):
    return a + b - 2 * a * b


def body(
    q_ref,
    k_ref,
    v_ref,
    do_ref,
    moe_ref,
    ids_ref,
    gw_ref,
    sg_ref,
    su_ref,
    w_ref,
    dq_ref,
    dk_ref,
    dv_ref,
    gg_ref,
    gp_ref,
    up_ref,
    kv,
    qd,
    qd_send,
    probs,
    dprob,
    maxes,
    stats,
    dq_acc,
    dkv,
    dqs,
    dq_recv,
    merge_recv,
    e1_recv,
    e2_send,
    e2_recv,
    total,
    ebk,
    ebv,
    moe,
    send_rows,
    recv_rows,
    onehot,
    score_send,
    score_recv,
    sg,
    su,
    gp,
    up,
    dk_out,
    dv_out,
    gg_out,
    w_buf,
    w_sem,
    in_sem,
    out_sem,
    a_sem,
    s1_sem,
    s2_sem,
    relay_sem,
    c_sem,
    d_sem,
    merge_sem,
    e1_sem,
    e2_sem,
    ebk_sem,
    ebv_sem,
    score_sem,
):
    c = lax.axis_index("ctx")
    e = lax.axis_index("exp")
    rows = k_ref.shape[0]
    sub = rows // 2
    heads = q_ref.shape[1] // HEAD
    width = heads * sub
    tokens, model = moe_ref.shape
    slots, hidden = sg_ref.shape
    z_hi, x, core = c // 8, (c // 2) % 4, c % 2
    chip = c // 2
    y, z_lo = e // 2, e % 2
    y_half = y % 2
    kv_head = e // 4

    def far_z(t):
        return t // 4

    def shift(t):
        m = t % 4
        return m + m // 2 - 2 * (m // 3)

    def from_chip(t):
        return flip(z_hi, far_z(t)) * 4 + (x + 4 - shift(t)) % 4

    def to_chip(t):
        return flip(z_hi, far_z(t)) * 4 + (x + shift(t)) % 4

    def to_device(t):
        return (to_chip(t) * 2 + core, y * 2 + flip(z_lo, far_z(t)))

    other_core = (c + 1 - 2 * core, e)
    partner = (15 - c, y * 2 + 1 - z_lo)
    z_mate = (c, y * 2 + 1 - z_lo)
    y_mate = (c, (y + 1 - 2 * y_half) * 2 + z_lo)

    def remote(src, dst, send_sem, recv_sem, device):
        return pltpu.make_async_remote_copy(
            src_ref=src,
            dst_ref=dst,
            send_sem=send_sem,
            recv_sem=recv_sem,
            device_id=device,
            device_id_type=MESH,
        )

    def half(index):
        return pl.ds(pl.multiple_of(index * sub, sub), sub)

    barrier = pltpu.get_barrier_semaphore()
    peers = [to_device(t) for t in range(1, 8)]
    peers += [(c, (e + step) % 8) for step in range(1, 8)]
    peers += [other_core, partner]
    for peer in peers:
        pl.semaphore_signal(barrier, inc=1, device_id=peer, device_id_type=MESH)

    head_cols = pl.ds(pl.multiple_of(kv_head * HEAD, HEAD), HEAD)
    pairs = [
        (k_ref.at[:, head_cols], kv.at[core, chip, 0]),
        (v_ref.at[:, head_cols], kv.at[core, chip, 1]),
    ]
    for n, ref in enumerate((q_ref, do_ref)):
        for h in range(heads):
            cols = pl.ds(h * HEAD, HEAD)
            pairs.append((ref.at[pl.ds(sub, sub), cols], qd_send.at[n, pl.ds(h * sub, sub), :]))
    for n, ref in enumerate((q_ref, do_ref)):
        for h in range(heads):
            cols = pl.ds(h * HEAD, HEAD)
            pairs.append((ref.at[pl.ds(0, sub), cols], qd.at[0, n, pl.ds(h * sub, sub), :]))
    pairs += [(moe_ref, moe), (sg_ref, sg), (su_ref, su)]
    loads = [
        pltpu.make_async_copy(src, dst, in_sem.at[n]) for n, (src, dst) in enumerate(pairs)
    ]
    for load in loads[: 2 + 2 * heads]:
        load.start()

    chunk = w_buf.shape[1]
    chunks = hidden // chunk

    def weight_copy(i, slot):
        return pltpu.make_async_copy(
            w_ref.at[0, pl.ds(pl.multiple_of(i * chunk, chunk), chunk), :],
            w_buf.at[slot],
            w_sem.at[slot],
        )

    for load in loads[: 2 + 2 * heads]:
        load.wait()
    pl.semaphore_wait(barrier, len(peers))

    c_copy = remote(qd_send, qd.at[1], c_sem.at[0], c_sem.at[1], partner)

    def first_hop(t, n):
        if isinstance(t, int) and t > 4:
            block, index = from_chip(4), 1 - z_lo if n == 0 else y_half
            device = ((chip - x + (x + shift(t)) % 4) * 2 + core, e)
        else:
            block, index = chip, z_lo if n == 0 else y_half
            device = to_device(t)
        piece = kv.at[core, block, n, half(index), :]
        return remote(piece, piece, s1_sem.at[0, t, n], s1_sem.at[1, t, n], device)

    def second_hop(t, n):
        index = flip(z_lo, far_z(t)) if n == 0 else y_half
        piece = kv.at[core, from_chip(t), n, half(index), :]
        mate = z_mate if n == 0 else y_mate
        return remote(piece, piece, s2_sem.at[0, t, n], s2_sem.at[1, t, n], mate)

    def relay(t):
        block = kv.at[core, from_chip(t)]
        return remote(block, block, relay_sem.at[0, t], relay_sem.at[1, t], other_core)

    for n in range(2):
        first_hop(4, n).start()
    c_copy.start()
    for t in range(1, 4):
        for n in range(2):
            first_hop(t, n).start()
    relay(0).start()
    weight_copy(0, 0).start()
    weight_copy(1, 1).start()
    for load in loads[2 + 2 * heads :]:
        load.start()

    slot_row = lax.broadcasted_iota(jnp.int32, (slots, tokens), 0)
    slot_expert = slot_row // CAP
    ids = ids_ref[...]
    weights = gw_ref[...].astype(jnp.float32)
    match = jnp.zeros((slots, tokens), jnp.float32)
    weight_of = jnp.zeros((slots, tokens), jnp.float32)
    for k in range(TOPK):
        hit = ids[k : k + 1, :] == slot_expert
        match = jnp.where(hit, 1.0, match)
        weight_of = jnp.where(hit, weights[k : k + 1, :], weight_of)
    row = lax.broadcasted_iota(jnp.int32, (tokens, tokens), 0)
    col = lax.broadcasted_iota(jnp.int32, (tokens, tokens), 1)
    earlier = jnp.where(row < col, 1.0, 0.0).astype(jnp.bfloat16)
    rank = dot(match.astype(jnp.bfloat16), earlier, NN)
    place = jnp.where(rank == (slot_row % CAP).astype(jnp.float32), match, 0.0)
    onehot[...] = place
    place_b = place.astype(jnp.bfloat16)
    for load in loads[2 + 2 * heads :]:
        load.wait()
    step_cols = 512

    def gather_cols(i, carry):
        cols = pl.ds(pl.multiple_of(i * step_cols, step_cols), step_cols)
        send_rows[:, cols] = dot(place_b, moe[:, cols], NN).astype(jnp.bfloat16)
        return carry

    lax.fori_loop(0, model // step_cols, gather_cols, 0)
    slot_weight = dot(
        (place * weight_of).astype(jnp.bfloat16), jnp.ones((tokens, HEAD), jnp.bfloat16), NN
    )
    send_rows[:, model : model + HEAD] = slot_weight.astype(jnp.bfloat16)
    own_rows = pl.ds(pl.multiple_of(e * CAP, CAP), CAP)

    def far_rows(far):
        return pl.ds(pl.multiple_of(far * CAP, CAP), CAP)

    a_copies = []
    for step in range(1, 8):
        far = (e + step) % 8
        copy = remote(
            send_rows.at[far_rows(far), :],
            recv_rows.at[own_rows, :],
            a_sem.at[0, step - 1],
            a_sem.at[1, step - 1],
            (c, far),
        )
        copy.start()
        a_copies.append(copy)
    recv_rows[own_rows, :] = send_rows[own_rows, :]

    dkv[...] = jnp.zeros_like(dkv)
    dq_acc[...] = jnp.zeros_like(dq_acc)
    for s in range(2):
        stats[s, 0:1, :] = jnp.full((1, width), -1e30, jnp.float32)
        stats[s, 1:3, :] = jnp.zeros((2, width), jnp.float32)

    def sub_of(s):
        return 2 * c + s * (31 - 4 * c)

    def last_of(s):
        return c + s * (15 - 2 * c)

    def first(s, p, block, masked):
        j = 2 * block + p
        place_at = s * (c + 1) + j
        m, l, d = stats[s, 0:1, :], stats[s, 1:2, :], stats[s, 2:3, :]
        scores = dot(kv[p, block, 0], qd[s, 0], NT) * (SCALE * LOG2E)
        dp = dot(kv[p, block, 1], qd[s, 1], NT)
        if masked:
            key_at = lax.broadcasted_iota(jnp.int32, (rows, width), 0) + j * rows
            query_at = lax.broadcasted_iota(jnp.int32, (rows, width), 1) % sub + sub_of(s) * sub
            scores = jnp.where(key_at <= query_at, scores, -jnp.inf)
        new = jnp.maximum(m, jnp.max(scores, axis=0, keepdims=True))
        factor = jnp.exp2(m - new)
        ex = jnp.exp2(scores - new)
        stats[s, 0:1, :] = new
        stats[s, 1:2, :] = l * factor + jnp.sum(ex, axis=0, keepdims=True)
        stats[s, 2:3, :] = d * factor + jnp.sum(ex * dp, axis=0, keepdims=True)
        probs[place_at] = ex.astype(probs.dtype)
        dprob[place_at] = dp
        maxes[place_at] = jnp.broadcast_to(new, (8, width))

    def second(s, p, block):
        j = 2 * block + p
        place_at = s * (c + 1) + j
        scale = jnp.exp2(maxes[place_at][0:1] - stats[s, 0:1, :]) * stats[s, 1:2, :]
        pr = probs[place_at].astype(jnp.float32) * scale
        ds = pr * (dprob[place_at] - stats[s, 2:3, :])
        p_b = pr.astype(jnp.bfloat16)
        ds_b = ds.astype(jnp.bfloat16)
        dkv[p, block, 0] += dot(ds_b, qd[s, 0], NN)
        dkv[p, block, 1] += dot(p_b, qd[s, 1], NN)
        dq_acc[s] += dot(kv[p, block, 0], ds_b, TN)

    def arrive(t):
        for n in range(2):
            first_hop(t, n).wait_recv()
            second_hop(t, n).start()

    def complete(t):
        for n in range(2):
            second_hop(t, n).wait_recv()
        relay(t).start()

    arrive(4)
    for t in range(5, 8):
        for n in range(2):
            first_hop(t, n).start()
    arrive(1)
    c_copy.wait()

    def first_step(t, carry):
        @pl.when((t + 2 < 8) & (t != 2))
        def _():
            arrive(t + 2)

        @pl.when(t + 1 < 8)
        def _():
            complete(t + 1)

        relay(t).wait_recv()
        block = from_chip(t)

        def tile(i, inner):
            s, p = i % 2, i // 2
            j = 2 * block + p

            @pl.when(j < last_of(s))
            def _():
                first(s, p, block, False)

            @pl.when(j == last_of(s))
            def _():
                first(s, p, block, True)

            return inner

        lax.fori_loop(0, 4, tile, 0)
        return carry

    lax.fori_loop(0, 8, first_step, 0)
    relay(0).wait_send()
    for t in range(1, 8):
        for n in range(2):
            first_hop(t, n).wait_send()
            second_hop(t, n).wait_send()
        relay(t).wait_send()

    for s in range(2):
        inverse = 1.0 / stats[s, 1:2, :]
        stats[s, 1:2, :] = inverse
        stats[s, 2:3, :] = stats[s, 2:3, :] * inverse

    far_core = 1 - core

    def merge(t):
        return remote(
            kv.at[far_core, to_chip(7 - t)],
            merge_recv.at[t],
            merge_sem.at[0, t],
            merge_sem.at[1, t],
            other_core,
        )

    def kept(t, n):
        return flip(z_lo, far_z(7 - t)) if n == 0 else y_half

    def mate_copy(t, n):
        return remote(
            kv.at[core, to_chip(7 - t), n, half(1 - kept(t, n)), :],
            e1_recv.at[t, n],
            e1_sem.at[0, t, n],
            e1_sem.at[1, t, n],
            z_mate if n == 0 else y_mate,
        )

    def ctx_copy(t):
        return remote(
            e2_send.at[t], e2_recv.at[t], e2_sem.at[0, t], e2_sem.at[1, t], to_device(7 - t)
        )

    def after_merge(t):
        block = to_chip(7 - t)
        merge(t).wait_recv()
        for n in range(2):
            there, here = half(1 - kept(t, n)), half(kept(t, n))
            kv[core, block, n, there, :] = (
                dkv[core, block, n, there, :] + merge_recv[t, n, there, :].astype(jnp.float32)
            ).astype(jnp.bfloat16)
            mate_copy(t, n).start()
            dkv[core, block, n, here, :] += merge_recv[t, n, here, :].astype(jnp.float32)

    def mate_sum(t, n):
        mate_copy(t, n).wait_recv()
        return dkv[core, to_chip(7 - t), n, half(kept(t, n)), :] + e1_recv[t, n].astype(
            jnp.float32
        )

    def after_mate(t):
        for n in range(2):
            e2_send[t, n] = mate_sum(t, n).astype(jnp.bfloat16)
        ctx_copy(t).start()

    def second_step(t, carry):
        block = to_chip(7 - t)

        def tile(i, inner):
            s, p = i % 2, i // 2

            @pl.when(2 * block + p <= last_of(s))
            def _():
                second(s, p, block)

            return inner

        lax.fori_loop(0, 4, tile, 0)
        kv[far_core, block] = dkv[far_core, block].astype(jnp.bfloat16)
        merge(t).start()

        @pl.when(t >= 2)
        def _():
            after_merge(t - 2)

        @pl.when(t >= 5)
        def _():
            after_mate(t - 5)

        return carry

    lax.fori_loop(0, 8, second_step, 0)
    after_merge(6)
    for s in range(2):
        dqs[s] = (dq_acc[s] * SCALE).T.astype(jnp.bfloat16)
    d_copy = remote(dqs.at[1], dq_recv, d_sem.at[0], d_sem.at[1], partner)
    d_copy.start()
    outs = []

    def store(src, dst):
        copy = pltpu.make_async_copy(src, dst, out_sem.at[len(outs)])
        copy.start()
        outs.append(copy)

    for h in range(heads):
        store(
            dqs.at[0, pl.ds(h * sub, sub), :], dq_ref.at[pl.ds(0, sub), pl.ds(h * HEAD, HEAD)]
        )
    after_mate(3)
    after_merge(7)
    for t in range(4, 7):
        after_mate(t)

    for copy in a_copies:
        copy.wait()
    weight_col = recv_rows[:, model : model + HEAD].astype(jnp.float32)
    weight_wide = jnp.concatenate([weight_col] * (chunk // HEAD), axis=1)

    def expert_step(i, score):
        slot = i % 2
        weight_copy(i, slot).wait()
        cols = pl.ds(pl.multiple_of(i * chunk, chunk), chunk)
        back = dot(recv_rows[:, 0:model], w_buf[slot], NT)

        @pl.when(i + 2 < chunks)
        def _():
            weight_copy(i + 2, slot).start()

        g = sg[:, cols].astype(jnp.float32)
        u = su[:, cols].astype(jnp.float32)
        sig = 1.0 / (1.0 + jnp.exp(-g))
        silu = g * sig
        act = (silu * u).astype(jnp.bfloat16).astype(jnp.float32)
        act_grad = weight_wide * back
        gp[:, cols] = (act_grad * u * sig * (1.0 + g * (1.0 - sig))).astype(jnp.bfloat16)
        up[:, cols] = (act_grad * silu).astype(jnp.bfloat16)
        return score + jnp.sum(act * back, axis=1, keepdims=True)

    score = lax.fori_loop(0, chunks, expert_step, jnp.zeros((slots, 1), jnp.float32))
    score_send[...] = jnp.broadcast_to(score, (slots, HEAD))
    score_copies = []
    for step in range(1, 8):
        far = (e + step) % 8
        copy = remote(
            score_send.at[far_rows(far), :],
            score_recv.at[own_rows, :],
            score_sem.at[0, step - 1],
            score_sem.at[1, step - 1],
            (c, far),
        )
        copy.start()
        score_copies.append(copy)
    score_recv[own_rows, :] = score_send[own_rows, :]
    store(gp, gp_ref)
    store(up, up_ref)

    for n in range(2):
        total[n] = mate_sum(7, n)
    for t in range(7):
        ctx_copy(t).wait_recv()
        total[...] += e2_recv[t].astype(jnp.float32)
    part = rows // 8

    def owner_copy(n, i):
        rows_i = pl.ds(i * part, part)
        if n == 0:
            return remote(
                total.at[0, rows_i, :], ebk.at[y], ebk_sem.at[0, i], ebk_sem.at[1, y], (c, 4 * z_lo + i)
            )
        source = (y // 2) * 2 + z_lo
        return remote(
            total.at[1, rows_i, :],
            ebv.at[source],
            ebv_sem.at[0, i],
            ebv_sem.at[1, source],
            (c, 4 * y_half + i),
        )

    def owner_of(n, i):
        return 4 * (z_lo if n == 0 else y_half) + i

    for n in range(2):
        for i in range(4):

            @pl.when(owner_of(n, i) != e)
            def _():
                owner_copy(n, i).start()

            @pl.when(owner_of(n, i) == e)
            def _():
                if n == 0:
                    ebk[y] = total[0, i * part : (i + 1) * part, :]
                else:
                    ebv[(y // 2) * 2 + z_lo] = total[1, i * part : (i + 1) * part, :]

    for copy in score_copies:
        copy.wait()
    picked = onehot[...] * score_recv[...]
    for k in range(TOPK):
        gg_out[k : k + 1, :] = jnp.sum(
            jnp.where(ids[k : k + 1, :] == slot_expert, picked, 0.0), axis=0, keepdims=True
        )
    store(gg_out, gg_ref)

    d_copy.wait()
    for h in range(heads):
        store(
            dq_recv.at[pl.ds(h * sub, sub), :],
            dq_ref.at[pl.ds(sub, sub), pl.ds(h * HEAD, HEAD)],
        )

    for i in range(4):
        source_k = 2 * i + e // 4
        source_v = (2 * (i // 2) + e // 4) * 2 + i % 2

        @pl.when(source_k != e)
        def _():
            remote(ebk.at[i], ebk.at[i], ebk_sem.at[0, i], ebk_sem.at[1, i], other_core).wait_recv()

        @pl.when(source_v != e)
        def _():
            remote(ebv.at[i], ebv.at[i], ebv_sem.at[0, i], ebv_sem.at[1, i], other_core).wait_recv()

    for kv_index in range(KVHEADS):
        cols = slice(kv_index * HEAD, (kv_index + 1) * HEAD)
        first_source = 2 * kv_index
        dk_out[:, cols] = ((ebk[first_source] + ebk[first_source + 1]) * SCALE).astype(jnp.bfloat16)
        dv_out[:, cols] = (ebv[first_source] + ebv[first_source + 1]).astype(jnp.bfloat16)
    store(dk_out, dk_ref)
    store(dv_out, dv_ref)

    for t in range(8):
        merge(t).wait_send()
        for n in range(2):
            mate_copy(t, n).wait_send()
        if t < 7:
            ctx_copy(t).wait_send()
    for n in range(2):
        for i in range(4):

            @pl.when(owner_of(n, i) != e)
            def _():
                owner_copy(n, i).wait_send()

    for copy in outs:
        copy.wait()


def hand_on(*refs):
    count = len(refs) // 2
    for n in range(count):
        refs[count + n][...] = refs[n][...]


def shards(
    queries,
    keys,
    values,
    out_grad,
    moe_grad,
    expert_ids,
    gate_weights,
    saved_gate,
    saved_up,
    down_weight,
):
    rows, columns = queries.shape
    sub = rows // 2
    width = columns // HEAD * sub
    tokens, model = moe_grad.shape
    slots, hidden = saved_gate.shape
    bf16, f32 = jnp.bfloat16, jnp.float32
    vmem = pl.BlockSpec(memory_space=pltpu.VMEM)
    hbm = pl.BlockSpec(memory_space=pl.ANY)
    dma = pltpu.SemaphoreType.DMA
    shapes = (
        jax.ShapeDtypeStruct((rows, columns), bf16),
        jax.ShapeDtypeStruct((rows // 8, KVHEADS * HEAD), bf16),
        jax.ShapeDtypeStruct((rows // 8, KVHEADS * HEAD), bf16),
        jax.ShapeDtypeStruct((TOPK, tokens), f32),
        jax.ShapeDtypeStruct((slots, hidden), bf16),
        jax.ShapeDtypeStruct((slots, hidden), bf16),
    )
    results = pl.pallas_call(
        body,
        out_shape=shapes,
        in_specs=[hbm] * 5 + [vmem] * 2 + [hbm] * 3,
        out_specs=(hbm,) * 6,
        scratch_shapes=[
            pltpu.VMEM((2, 8, 2, rows, HEAD), bf16),
            pltpu.VMEM((2, 2, width, HEAD), bf16),
            pltpu.VMEM((2, width, HEAD), bf16),
            pltpu.VMEM((17, rows, width), bf16),
            pltpu.VMEM((17, rows, width), f32),
            pltpu.VMEM((17, 8, width), f32),
            pltpu.VMEM((2, 8, width), f32),
            pltpu.VMEM((2, HEAD, width), f32),
            pltpu.VMEM((2, 8, 2, rows, HEAD), f32),
            pltpu.VMEM((2, width, HEAD), bf16),
            pltpu.VMEM((width, HEAD), bf16),
            pltpu.VMEM((8, 2, rows, HEAD), bf16),
            pltpu.VMEM((8, 2, sub, HEAD), bf16),
            pltpu.VMEM((7, 2, sub, HEAD), bf16),
            pltpu.VMEM((7, 2, sub, HEAD), bf16),
            pltpu.VMEM((2, sub, HEAD), f32),
            pltpu.VMEM((4, rows // 8, HEAD), f32),
            pltpu.VMEM((4, rows // 8, HEAD), f32),
            pltpu.VMEM((tokens, model), bf16),
            pltpu.VMEM((slots, model + HEAD), bf16),
            pltpu.VMEM((slots, model + HEAD), bf16),
            pltpu.VMEM((slots, tokens), f32),
            pltpu.VMEM((slots, HEAD), f32),
            pltpu.VMEM((slots, HEAD), f32),
            pltpu.VMEM((slots, hidden), bf16),
            pltpu.VMEM((slots, hidden), bf16),
            pltpu.VMEM((slots, hidden), bf16),
            pltpu.VMEM((slots, hidden), bf16),
            pltpu.VMEM((rows // 8, KVHEADS * HEAD), bf16),
            pltpu.VMEM((rows // 8, KVHEADS * HEAD), bf16),
            pltpu.VMEM((TOPK, tokens), f32),
            pltpu.VMEM((2, 256, model), bf16),
            dma((2,)),
            dma((21,)),
            dma((13,)),
            dma((2, 7)),
            dma((2, 8, 2)),
            dma((2, 8, 2)),
            dma((2, 8)),
            dma((2,)),
            dma((2,)),
            dma((2, 8)),
            dma((2, 8, 2)),
            dma((2, 7)),
            dma((2, 4)),
            dma((2, 4)),
            dma((2, 7)),
        ],
        compiler_params=pltpu.CompilerParams(
            collective_id=0, has_side_effects=True, vmem_limit_bytes=61 * 1024 * 1024
        ),
    )(
        queries,
        keys,
        values,
        out_grad,
        moe_grad,
        expert_ids.T,
        gate_weights.T,
        saved_gate,
        saved_up,
        down_weight,
    )
    results = pl.pallas_call(
        hand_on,
        out_shape=shapes,
        in_specs=[vmem] * 6,
        out_specs=(vmem,) * 6,
    )(*results)
    return results[0], results[1], results[2], results[3].T, results[4], results[5]


def solution(mesh):
    both = ("ctx", "exp")
    in_specs = (
        P("ctx", "exp"),
        P("ctx", None),
        P("ctx", None),
        P("ctx", "exp"),
        P(both, None),
        P(both, None),
        P(both, None),
        P(both, None),
        P(both, None),
        P("exp", None, None),
    )
    out_specs = (
        P("ctx", "exp"),
        P(both, None),
        P(both, None),
        P(both, None),
        P(both, None),
        P(both, None),
    )
    return jax.shard_map(shards, mesh=mesh, in_specs=in_specs, out_specs=out_specs, check_vma=False)
```

time: 106 us -> 83.6 us (0.79); the launches traced: 104 us -> 83.4 us
  local copies, waits for them, and re-layouts: 12.3 us -> 0 us
  Pallas kernels: 91.6 us -> 82.7 us
    unnamed x7 -> x0, local copies, waits for them, and re-layouts: 10.8 us -> none
    pallas_call x1 -> x2, Pallas kernels: 91.6 us -> 82.7 us  [the longest x1 80.4 us: shards(): pl.pallas_call(body, out_shape=shapes, in_specs=[hbm] * 5 + [vmem] * 2 +...]
    pallas_call x1 -> x0, local copies, waits for them, and re-layouts: 1.5 us -> none  [shards(): pl.pallas_call(body, out_shape=(jax.ShapeDtypeStruct((rows, columns), bf1...]
where the time goes in v2:
time: 83.6 us; the launch traced here: 83.4 us
  Pallas kernels  82.7 us (99%)
    pallas_call x1, Pallas kernels, shards(): pl.pallas_call(body, out_shape=shapes, in_specs=[hbm] * 5 + [vmem] * 2 +...  80.4 us
    pallas_call x1, Pallas kernels, shards(): pl.pallas_call(hand_on, out_shape=shapes, in_specs=[vmem] * 6, out_specs=...  2.32 us

profile of v2, /device:TPU:0, one launch (start us, length us, event | category | flops | bytes accessed | tf_op | source)
XLA Modules:
  0.0 83.4 jit_solution(3523039549299834384)
XLA Ops:
  0.6 80.4 %shard_map.145 = (bf16[384,512]{1,0:T(8,128)(2,1)}, bf16[48,256]{1,0:T(8,128)(2,1)}, bf16[48,256]{1,0:T(8,128)(2,1)}, f32[8,128]{1,0:T(8,128)}, bf16[128,1536]{1,0:T(8,128)(2,1)}, /*index=5*/bf16[128,1536]{1,0:T(8,128)(2,1)}) custom-call(bf16[384,512]{1,0:T(8,128)(2,1)} %q_ref.1, bf16[384,256]{1,0:T(8,128)(2,1)} %k_ref.1, bf16[384,256]{1,0:T(8,128)(2,1)} %v_ref.1, ...), custom_call_target="tpu_custom_call" | custom-call | tf_op jit(solution)/shard_map/pallas_call | solution.py:637
  81.0 2.3 %shard_map.146 = (bf16[384,512]{1,0:T(8,128)(2,1)}, bf16[48,256]{1,0:T(8,128)(2,1)}, bf16[48,256]{1,0:T(8,128)(2,1)}, f32[8,128]{1,0:T(8,128)}, bf16[128,1536]{1,0:T(8,128)(2,1)}, /*index=5*/bf16[128,1536]{1,0:T(8,128)(2,1)}) custom-call(bf16[384,512]{1,0:T(8,128)(2,1)} %get-tuple-element.18.refs_0_, bf16[48,256]{1,0:T(8,128)(2,1)} %get-tuple-element.19.refs_1_, ...), custom_call_target="tpu_custom_call" | custom-call | tf_op jit(solution)/shard_map/pallas_call | solution.py:706

commit v3 on v2

--- a/solution.py
+++ b/solution.py
@@ -139,7 +139,7 @@
         return pl.ds(pl.multiple_of(index * sub, sub), sub)
 
     barrier = pltpu.get_barrier_semaphore()
-    peers = [to_device(t) for t in range(1, 8)]
+    peers = [to_device(t) for t in range(1, 5)]
     peers += [(c, (e + step) % 8) for step in range(1, 8)]
     peers += [other_core, partner]
     for peer in peers:
@@ -164,6 +164,7 @@
     ]
     for load in loads[: 2 + 2 * heads]:
         load.start()
+    loads[2 + 4 * heads].start()
 
     chunk = w_buf.shape[1]
     chunks = hidden // chunk
@@ -175,11 +176,28 @@
             w_sem.at[slot],
         )
 
+    dkv[...] = jnp.zeros_like(dkv)
+    dq_acc[...] = jnp.zeros_like(dq_acc)
+    for s in range(2):
+        stats[s, 0:1, :] = jnp.full((1, width), -1e30, jnp.float32)
+        stats[s, 1:3, :] = jnp.zeros((2, width), jnp.float32)
+
     for load in loads[: 2 + 2 * heads]:
         load.wait()
     pl.semaphore_wait(barrier, len(peers))
 
-    c_copy = remote(qd_send, qd.at[1], c_sem.at[0], c_sem.at[1], partner)
+    wide = width // 2
+
+    def exchange(part, n):
+        piece = pl.ds(part * wide, wide)
+        return remote(
+            qd_send.at[n, piece, :],
+            qd.at[1, n, piece, :],
+            c_sem.at[0, part, n],
+            c_sem.at[1, part, n],
+            partner,
+        )
+
 
     def first_hop(t, n):
         if isinstance(t, int) and t > 4:
@@ -203,14 +221,13 @@
 
     for n in range(2):
         first_hop(4, n).start()
-    c_copy.start()
     for t in range(1, 4):
         for n in range(2):
             first_hop(t, n).start()
     relay(0).start()
     weight_copy(0, 0).start()
     weight_copy(1, 1).start()
-    for load in loads[2 + 2 * heads :]:
+    for load in loads[2 + 2 * heads : 2 + 4 * heads] + loads[3 + 4 * heads :]:
         load.start()
 
     slot_row = lax.broadcasted_iota(jnp.int32, (slots, tokens), 0)
@@ -230,8 +247,7 @@
     place = jnp.where(rank == (slot_row % CAP).astype(jnp.float32), match, 0.0)
     onehot[...] = place
     place_b = place.astype(jnp.bfloat16)
-    for load in loads[2 + 2 * heads :]:
-        load.wait()
+    loads[2 + 4 * heads].wait()
     step_cols = 512
 
     def gather_cols(i, carry):
@@ -259,53 +275,71 @@
             a_sem.at[1, step - 1],
             (c, far),
         )
-        copy.start()
         a_copies.append(copy)
     recv_rows[own_rows, :] = send_rows[own_rows, :]
 
-    dkv[...] = jnp.zeros_like(dkv)
-    dq_acc[...] = jnp.zeros_like(dq_acc)
-    for s in range(2):
-        stats[s, 0:1, :] = jnp.full((1, width), -1e30, jnp.float32)
-        stats[s, 1:3, :] = jnp.zeros((2, width), jnp.float32)
-
     def sub_of(s):
         return 2 * c + s * (31 - 4 * c)
 
     def last_of(s):
         return c + s * (15 - 2 * c)
 
-    def first(s, p, block, masked):
-        j = 2 * block + p
-        place_at = s * (c + 1) + j
-        m, l, d = stats[s, 0:1, :], stats[s, 1:2, :], stats[s, 2:3, :]
-        scores = dot(kv[p, block, 0], qd[s, 0], NT) * (SCALE * LOG2E)
-        dp = dot(kv[p, block, 1], qd[s, 1], NT)
-        if masked:
-            key_at = lax.broadcasted_iota(jnp.int32, (rows, width), 0) + j * rows
-            query_at = lax.broadcasted_iota(jnp.int32, (rows, width), 1) % sub + sub_of(s) * sub
-            scores = jnp.where(key_at <= query_at, scores, -jnp.inf)
-        new = jnp.maximum(m, jnp.max(scores, axis=0, keepdims=True))
+    def last_pair(s):
+        return last_of(s) // 2
+
+    def first(s, block, cols, masked):
+        place_at = 2 * (s * (c // 2 + 1) + block)
+        m, l, d = stats[s, 0:1, cols], stats[s, 1:2, cols], stats[s, 2:3, cols]
+        count = cols.stop - cols.start
+        new = m
+        scores, dprobs = [], []
+        for p in range(2):
+            sc = dot(kv[p, block, 0], qd[s, 0, cols, :], NT) * (SCALE * LOG2E)
+            if masked:
+                key_at = lax.broadcasted_iota(jnp.int32, (rows, count), 0)
+                query_at = lax.broadcasted_iota(jnp.int32, (rows, count), 1) % sub
+                offset = sub_of(s) * sub - (2 * block + p) * rows
+                sc = jnp.where(key_at - query_at <= offset, sc, -jnp.inf)
+            scores.append(sc)
+            dprobs.append(dot(kv[p, block, 1], qd[s, 1, cols, :], NT))
+            new = jnp.maximum(new, jnp.max(sc, axis=0, keepdims=True))
         factor = jnp.exp2(m - new)
-        ex = jnp.exp2(scores - new)
-        stats[s, 0:1, :] = new
-        stats[s, 1:2, :] = l * factor + jnp.sum(ex, axis=0, keepdims=True)
-        stats[s, 2:3, :] = d * factor + jnp.sum(ex * dp, axis=0, keepdims=True)
-        probs[place_at] = ex.astype(probs.dtype)
-        dprob[place_at] = dp
-        maxes[place_at] = jnp.broadcast_to(new, (8, width))
-
-    def second(s, p, block):
-        j = 2 * block + p
-        place_at = s * (c + 1) + j
-        scale = jnp.exp2(maxes[place_at][0:1] - stats[s, 0:1, :]) * stats[s, 1:2, :]
-        pr = probs[place_at].astype(jnp.float32) * scale
-        ds = pr * (dprob[place_at] - stats[s, 2:3, :])
-        p_b = pr.astype(jnp.bfloat16)
-        ds_b = ds.astype(jnp.bfloat16)
-        dkv[p, block, 0] += dot(ds_b, qd[s, 0], NN)
-        dkv[p, block, 1] += dot(p_b, qd[s, 1], NN)
-        dq_acc[s] += dot(kv[p, block, 0], ds_b, TN)
+        l = l * factor
+        d = d * factor
+        for p in range(2):
+            ex = jnp.exp2(scores[p] - new)
+            l = l + jnp.sum(ex, axis=0, keepdims=True)
+            d = d + jnp.sum(ex * dprobs[p], axis=0, keepdims=True)
+            probs[place_at + p, :, cols] = ex.astype(probs.dtype)
+            dprob[place_at + p, :, cols] = dprobs[p]
+        stats[s, 0:1, cols] = new
+        stats[s, 1:2, cols] = l
+        stats[s, 2:3, cols] = d
+        maxes[s * (c // 2 + 1) + block, :, cols] = jnp.broadcast_to(new, (8, count))
+
+    def first_pair(s, block, cols):
+        @pl.when(block < last_pair(s))
+        def _():
+            first(s, block, cols, False)
+
+        @pl.when(block == last_pair(s))
+        def _():
+            first(s, block, cols, True)
+
+    def second(s, block):
+        pair = s * (c // 2 + 1) + block
+        scale = jnp.exp2(maxes[pair][0:1] - stats[s, 0:1, :]) * stats[s, 1:2, :]
+        delta = stats[s, 2:3, :]
+        dq = dq_acc[s]
+        for p in range(2):
+            pr = probs[2 * pair + p].astype(jnp.float32) * scale
+            ds = pr * (dprob[2 * pair + p] - delta)
+            p_b = pr.astype(jnp.bfloat16)
+            ds_b = ds.astype(jnp.bfloat16)
+            dkv[p, block, 0] += dot(ds_b, qd[s, 0], NN)
+            dkv[p, block, 1] += dot(p_b, qd[s, 1], NN)
+            dq = dq + dot(kv[p, block, 0], ds_b, TN)
+        dq_acc[s] = dq
 
     def arrive(t):
         for n in range(2):
@@ -321,39 +355,63 @@
     for t in range(5, 8):
         for n in range(2):
             first_hop(t, n).start()
-    arrive(1)
-    c_copy.wait()
-
-    def first_step(t, carry):
-        @pl.when((t + 2 < 8) & (t != 2))
-        def _():
-            arrive(t + 2)
-
-        @pl.when(t + 1 < 8)
-        def _():
-            complete(t + 1)
-
-        relay(t).wait_recv()
+    for t in range(1, 4):
+        arrive(t)
+
+    for part in range(2):
+        for n in range(2):
+            exchange(part, n).start()
+
+    for load in loads[2 + 2 * heads : 2 + 4 * heads] + loads[3 + 4 * heads :]:
+        load.wait()
+
+    def first_step(i, carry):
+        far = i // 8
+        t = i % 4 + far * (4 + (i % 8) // 2 - i % 4)
+        s = (i // 4) % 2 + far * (i % 2 - (i // 4) % 2)
         block = from_chip(t)
 
-        def tile(i, inner):
-            s, p = i % 2, i // 2
-            j = 2 * block + p
-
-            @pl.when(j < last_of(s))
-            def _():
-                first(s, p, block, False)
-
-            @pl.when(j == last_of(s))
-            def _():
-                first(s, p, block, True)
-
-            return inner
-
-        lax.fori_loop(0, 4, tile, 0)
+        @pl.when((i >= 1) & (i < 4))
+        def _():
+            arrive(i + 4)
+
+        @pl.when(i < 7)
+        def _():
+            complete(i + 1)
+
+        @pl.when((i < 4) | ((i >= 8) & (i % 2 == 0)))
+        def _():
+            relay(t).wait_recv()
+
+        @pl.when(i == 4)
+        def _():
+            for n in range(2):
+                exchange(0, n).wait()
+
+        @pl.when(i == 7)
+        def _():
+            for copy in a_copies:
+                copy.start()
+
+        @pl.when(s == 0)
+        def _():
+            first_pair(0, block, slice(0, width))
+
+        @pl.when(s == 1)
+        def _():
+            first_pair(1, block, slice(0, wide))
+
         return carry
 
-    lax.fori_loop(0, 8, first_step, 0)
+    lax.fori_loop(0, 16, first_step, 0)
+    for n in range(2):
+        exchange(1, n).wait()
+
+    def first_rest(t, carry):
+        first_pair(1, t, slice(wide, width))
+        return carry
+
+    lax.fori_loop(0, 8, first_rest, 0)
     relay(0).wait_send()
     for t in range(1, 8):
         for n in range(2):
@@ -390,9 +448,11 @@
         )
 
     def ctx_copy(t):
-        return remote(
-            e2_send.at[t], e2_recv.at[t], e2_sem.at[0, t], e2_sem.at[1, t], to_device(7 - t)
-        )
+        if isinstance(t, int) and t == 3:
+            device = to_device(4)
+        else:
+            device = ((z_hi * 4 + (x + shift(7 - t)) % 4) * 2 + core, e)
+        return remote(e2_send.at[t], e2_recv.at[t], e2_sem.at[0, t], e2_sem.at[1, t], device)
 
     def after_merge(t):
         block = to_chip(7 - t)
@@ -416,19 +476,27 @@
             e2_send[t, n] = mate_sum(t, n).astype(jnp.bfloat16)
         ctx_copy(t).start()
 
+    def cross():
+        sums = [mate_sum(3, n) for n in range(2)]
+        for t in range(3):
+            ctx_copy(t).wait_recv()
+            for n in range(2):
+                sums[n] = sums[n] + e2_recv[t, n].astype(jnp.float32)
+        for n in range(2):
+            e2_send[3, n] = sums[n].astype(jnp.bfloat16)
+        ctx_copy(3).start()
+
     def second_step(t, carry):
         block = to_chip(7 - t)
 
-        def tile(i, inner):
-            s, p = i % 2, i // 2
-
-            @pl.when(2 * block + p <= last_of(s))
+        def tile(s, inner):
+            @pl.when(block <= last_pair(s))
             def _():
-                second(s, p, block)
+                second(s, block)
 
             return inner
 
-        lax.fori_loop(0, 4, tile, 0)
+        lax.fori_loop(0, 2, tile, 0)
         kv[far_core, block] = dkv[far_core, block].astype(jnp.bfloat16)
         merge(t).start()
 
@@ -436,18 +504,20 @@
         def _():
             after_merge(t - 2)
 
-        @pl.when(t >= 5)
-        def _():
-            after_mate(t - 5)
+        @pl.when((t >= 4) & (t < 7))
+        def _():
+            after_mate(t - 4)
 
         return carry
 
     lax.fori_loop(0, 8, second_step, 0)
+    for s in range(1, -1, -1):
+        dqs[s] = (dq_acc[s] * SCALE).T.astype(jnp.bfloat16)
+        if s == 1:
+            d_copy = remote(dqs.at[1], dq_recv, d_sem.at[0], d_sem.at[1], partner)
+            d_copy.start()
     after_merge(6)
-    for s in range(2):
-        dqs[s] = (dq_acc[s] * SCALE).T.astype(jnp.bfloat16)
-    d_copy = remote(dqs.at[1], dq_recv, d_sem.at[0], d_sem.at[1], partner)
-    d_copy.start()
+    after_mate(4)
     outs = []
 
     def store(src, dst):
@@ -459,10 +529,6 @@
         store(
             dqs.at[0, pl.ds(h * sub, sub), :], dq_ref.at[pl.ds(0, sub), pl.ds(h * HEAD, HEAD)]
         )
-    after_mate(3)
-    after_merge(7)
-    for t in range(4, 7):
-        after_mate(t)
 
     for copy in a_copies:
         copy.wait()
@@ -489,7 +555,13 @@
         up[:, cols] = (act_grad * silu).astype(jnp.bfloat16)
         return score + jnp.sum(act * back, axis=1, keepdims=True)
 
-    score = lax.fori_loop(0, chunks, expert_step, jnp.zeros((slots, 1), jnp.float32))
+    after_merge(7)
+    score = lax.fori_loop(0, 2, expert_step, jnp.zeros((slots, 1), jnp.float32))
+    cross()
+    after_mate(5)
+    score = lax.fori_loop(2, 4, expert_step, score)
+    after_mate(6)
+    score = lax.fori_loop(4, chunks, expert_step, score)
     score_send[...] = jnp.broadcast_to(score, (slots, HEAD))
     score_copies = []
     for step in range(1, 8):
@@ -509,7 +581,7 @@
 
     for n in range(2):
         total[n] = mate_sum(7, n)
-    for t in range(7):
+    for t in range(3, 7):
         ctx_copy(t).wait_recv()
         total[...] += e2_recv[t].astype(jnp.float32)
     part = rows // 8
@@ -643,9 +715,9 @@
             pltpu.VMEM((2, 8, 2, rows, HEAD), bf16),
             pltpu.VMEM((2, 2, width, HEAD), bf16),
             pltpu.VMEM((2, width, HEAD), bf16),
-            pltpu.VMEM((17, rows, width), bf16),
-            pltpu.VMEM((17, rows, width), f32),
-            pltpu.VMEM((17, 8, width), f32),
+            pltpu.VMEM((18, rows, width), bf16),
+            pltpu.VMEM((18, rows, width), f32),
+            pltpu.VMEM((9, 8, width), f32),
             pltpu.VMEM((2, 8, width), f32),
             pltpu.VMEM((2, HEAD, width), f32),
             pltpu.VMEM((2, 8, 2, rows, HEAD), f32),
@@ -679,7 +751,7 @@
             dma((2, 8, 2)),
             dma((2, 8, 2)),
             dma((2, 8)),
-            dma((2,)),
+            dma((2, 2, 2)),
             dma((2,)),
             dma((2, 8)),
             dma((2, 8, 2)),

time: 83.6 us -> 74.4 us (0.89)
  Pallas kernels: 82.7 us -> 73.5 us
    pallas_call x1, Pallas kernels: 80.4 us -> 71.2 us  [shards(): pl.pallas_call(body, out_shape=shapes, in_specs=[hbm] * 5 + [vmem] * 2 +...]
where the time goes in v3:
time: 74.4 us; the launch traced here: 74.1 us
  Pallas kernels  73.5 us (99%)
    pallas_call x1, Pallas kernels, shards(): pl.pallas_call(body, out_shape=shapes, in_specs=[hbm] * 5 + [vmem] * 2 +...  71.2 us
    pallas_call x1, Pallas kernels, shards(): pl.pallas_call(hand_on, out_shape=shapes, in_specs=[vmem] * 6, out_specs=...  2.32 us

profile of v3, /device:TPU:0, one launch (start us, length us, event | category | flops | bytes accessed | tf_op | source)
XLA Modules:
  0.0 74.1 jit_solution(5676216846971088659)
XLA Ops:
  0.6 71.2 %shard_map.145 = (bf16[384,512]{1,0:T(8,128)(2,1)}, bf16[48,256]{1,0:T(8,128)(2,1)}, bf16[48,256]{1,0:T(8,128)(2,1)}, f32[8,128]{1,0:T(8,128)}, bf16[128,1536]{1,0:T(8,128)(2,1)}, /*index=5*/bf16[128,1536]{1,0:T(8,128)(2,1)}) custom-call(bf16[384,512]{1,0:T(8,128)(2,1)} %q_ref.1, bf16[384,256]{1,0:T(8,128)(2,1)} %k_ref.1, bf16[384,256]{1,0:T(8,128)(2,1)} %v_ref.1, ...), custom_call_target="tpu_custom_call" | custom-call | tf_op jit(solution)/shard_map/pallas_call | solution.py:709
  71.8 2.3 %shard_map.146 = (bf16[384,512]{1,0:T(8,128)(2,1)}, bf16[48,256]{1,0:T(8,128)(2,1)}, bf16[48,256]{1,0:T(8,128)(2,1)}, f32[8,128]{1,0:T(8,128)}, bf16[128,1536]{1,0:T(8,128)(2,1)}, /*index=5*/bf16[128,1536]{1,0:T(8,128)(2,1)}) custom-call(bf16[384,512]{1,0:T(8,128)(2,1)} %get-tuple-element.18.refs_0_, bf16[48,256]{1,0:T(8,128)(2,1)} %get-tuple-element.19.refs_1_, ...), custom_call_target="tpu_custom_call" | custom-call | tf_op jit(solution)/shard_map/pallas_call | solution.py:778

commit v4 on v3

--- a/solution.py
+++ b/solution.py
@@ -52,7 +52,6 @@
     dq_acc,
     dkv,
     dqs,
-    dq_recv,
     merge_recv,
     e1_recv,
     e2_send,
@@ -233,33 +232,34 @@
     slot_row = lax.broadcasted_iota(jnp.int32, (slots, tokens), 0)
     slot_expert = slot_row // CAP
     ids = ids_ref[...]
-    weights = gw_ref[...].astype(jnp.float32)
-    match = jnp.zeros((slots, tokens), jnp.float32)
-    weight_of = jnp.zeros((slots, tokens), jnp.float32)
-    for k in range(TOPK):
-        hit = ids[k : k + 1, :] == slot_expert
-        match = jnp.where(hit, 1.0, match)
-        weight_of = jnp.where(hit, weights[k : k + 1, :], weight_of)
-    row = lax.broadcasted_iota(jnp.int32, (tokens, tokens), 0)
-    col = lax.broadcasted_iota(jnp.int32, (tokens, tokens), 1)
-    earlier = jnp.where(row < col, 1.0, 0.0).astype(jnp.bfloat16)
-    rank = dot(match.astype(jnp.bfloat16), earlier, NN)
-    place = jnp.where(rank == (slot_row % CAP).astype(jnp.float32), match, 0.0)
-    onehot[...] = place
-    place_b = place.astype(jnp.bfloat16)
-    loads[2 + 4 * heads].wait()
-    step_cols = 512
-
-    def gather_cols(i, carry):
-        cols = pl.ds(pl.multiple_of(i * step_cols, step_cols), step_cols)
-        send_rows[:, cols] = dot(place_b, moe[:, cols], NN).astype(jnp.bfloat16)
-        return carry
-
-    lax.fori_loop(0, model // step_cols, gather_cols, 0)
-    slot_weight = dot(
-        (place * weight_of).astype(jnp.bfloat16), jnp.ones((tokens, HEAD), jnp.bfloat16), NN
-    )
-    send_rows[:, model : model + HEAD] = slot_weight.astype(jnp.bfloat16)
+    def route():
+        weights = gw_ref[...].astype(jnp.float32)
+        match = jnp.zeros((slots, tokens), jnp.float32)
+        weight_of = jnp.zeros((slots, tokens), jnp.float32)
+        for k in range(TOPK):
+            hit = ids[k : k + 1, :] == slot_expert
+            match = jnp.where(hit, 1.0, match)
+            weight_of = jnp.where(hit, weights[k : k + 1, :], weight_of)
+        row = lax.broadcasted_iota(jnp.int32, (tokens, tokens), 0)
+        col = lax.broadcasted_iota(jnp.int32, (tokens, tokens), 1)
+        earlier = jnp.where(row < col, 1.0, 0.0).astype(jnp.bfloat16)
+        rank = dot(match.astype(jnp.bfloat16), earlier, NN)
+        place = jnp.where(rank == (slot_row % CAP).astype(jnp.float32), match, 0.0)
+        onehot[...] = place
+        place_b = place.astype(jnp.bfloat16)
+        loads[2 + 4 * heads].wait()
+        step_cols = 512
+
+        def gather_cols(i, carry):
+            cols = pl.ds(pl.multiple_of(i * step_cols, step_cols), step_cols)
+            send_rows[:, cols] = dot(place_b, moe[:, cols], NN).astype(jnp.bfloat16)
+            return carry
+
+        lax.fori_loop(0, model // step_cols, gather_cols, 0)
+        slot_weight = dot(
+            (place * weight_of).astype(jnp.bfloat16), jnp.ones((tokens, HEAD), jnp.bfloat16), NN
+        )
+        send_rows[:, model : model + HEAD] = slot_weight.astype(jnp.bfloat16)
     own_rows = pl.ds(pl.multiple_of(e * CAP, CAP), CAP)
 
     def far_rows(far):
@@ -276,7 +276,6 @@
             (c, far),
         )
         a_copies.append(copy)
-    recv_rows[own_rows, :] = send_rows[own_rows, :]
 
     def sub_of(s):
         return 2 * c + s * (31 - 4 * c)
@@ -385,13 +384,12 @@
 
         @pl.when(i == 4)
         def _():
+            route()
+            recv_rows[own_rows, :] = send_rows[own_rows, :]
+            for copy in a_copies:
+                copy.start()
             for n in range(2):
                 exchange(0, n).wait()
-
-        @pl.when(i == 7)
-        def _():
-            for copy in a_copies:
-                copy.start()
 
         @pl.when(s == 0)
         def _():
@@ -514,8 +512,18 @@
     for s in range(1, -1, -1):
         dqs[s] = (dq_acc[s] * SCALE).T.astype(jnp.bfloat16)
         if s == 1:
-            d_copy = remote(dqs.at[1], dq_recv, d_sem.at[0], d_sem.at[1], partner)
-            d_copy.start()
+            d_copies = [
+                remote(
+                    dqs.at[1, pl.ds(h * sub, sub), :],
+                    dq_ref.at[pl.ds(sub, sub), pl.ds(h * HEAD, HEAD)],
+                    d_sem.at[0, h],
+                    d_sem.at[1, h],
+                    partner,
+                )
+                for h in range(heads)
+            ]
+            for copy in d_copies:
+                copy.start()
     after_merge(6)
     after_mate(4)
     outs = []
@@ -627,13 +635,6 @@
         )
     store(gg_out, gg_ref)
 
-    d_copy.wait()
-    for h in range(heads):
-        store(
-            dq_recv.at[pl.ds(h * sub, sub), :],
-            dq_ref.at[pl.ds(sub, sub), pl.ds(h * HEAD, HEAD)],
-        )
-
     for i in range(4):
         source_k = 2 * i + e // 4
         source_v = (2 * (i // 2) + e // 4) * 2 + i % 2
@@ -667,7 +668,7 @@
             def _():
                 owner_copy(n, i).wait_send()
 
-    for copy in outs:
+    for copy in d_copies + outs:
         copy.wait()
 
 
@@ -722,7 +723,6 @@
             pltpu.VMEM((2, HEAD, width), f32),
             pltpu.VMEM((2, 8, 2, rows, HEAD), f32),
             pltpu.VMEM((2, width, HEAD), bf16),
-            pltpu.VMEM((width, HEAD), bf16),
             pltpu.VMEM((8, 2, rows, HEAD), bf16),
             pltpu.VMEM((8, 2, sub, HEAD), bf16),
             pltpu.VMEM((7, 2, sub, HEAD), bf16),
@@ -746,13 +746,13 @@
             pltpu.VMEM((2, 256, model), bf16),
             dma((2,)),
             dma((21,)),
-            dma((13,)),
+            dma((9,)),
             dma((2, 7)),
             dma((2, 8, 2)),
             dma((2, 8, 2)),
             dma((2, 8)),
             dma((2, 2, 2)),
-            dma((2,)),
+            dma((2, columns // HEAD)),
             dma((2, 8)),
             dma((2, 8, 2)),
             dma((2, 7)),

time: 74.4 us -> 72.2 us (0.970); the launches traced: 74.1 us -> 70.8 us
  Pallas kernels: 73.5 us -> 70.1 us
    pallas_call x1, Pallas kernels: 71.2 us -> 67.8 us  [shards(): pl.pallas_call(body, out_shape=shapes, in_specs=[hbm] * 5 + [vmem] * 2 +...]
where the time goes in v4:
time: 72.2 us; the launch traced here: 70.8 us
  Pallas kernels  70.1 us (97%)
    pallas_call x1, Pallas kernels, shards(): pl.pallas_call(body, out_shape=shapes, in_specs=[hbm] * 5 + [vmem] * 2 +...  67.8 us
    pallas_call x1, Pallas kernels, shards(): pl.pallas_call(hand_on, out_shape=shapes, in_specs=[vmem] * 6, out_specs=...  2.32 us

profile of v4, /device:TPU:0, one launch (start us, length us, event | category | flops | bytes accessed | tf_op | source)
XLA Modules:
  0.0 70.8 jit_solution(12739524225201308284)
XLA Ops:
  0.6 67.8 %shard_map.145 = (bf16[384,512]{1,0:T(8,128)(2,1)}, bf16[48,256]{1,0:T(8,128)(2,1)}, bf16[48,256]{1,0:T(8,128)(2,1)}, f32[8,128]{1,0:T(8,128)}, bf16[128,1536]{1,0:T(8,128)(2,1)}, /*index=5*/bf16[128,1536]{1,0:T(8,128)(2,1)}) custom-call(bf16[384,512]{1,0:T(8,128)(2,1)} %q_ref.1, bf16[384,256]{1,0:T(8,128)(2,1)} %k_ref.1, bf16[384,256]{1,0:T(8,128)(2,1)} %v_ref.1, ...), custom_call_target="tpu_custom_call" | custom-call | tf_op jit(solution)/shard_map/pallas_call | solution.py:710
  68.5 2.3 %shard_map.146 = (bf16[384,512]{1,0:T(8,128)(2,1)}, bf16[48,256]{1,0:T(8,128)(2,1)}, bf16[48,256]{1,0:T(8,128)(2,1)}, f32[8,128]{1,0:T(8,128)}, bf16[128,1536]{1,0:T(8,128)(2,1)}, /*index=5*/bf16[128,1536]{1,0:T(8,128)(2,1)}) custom-call(bf16[384,512]{1,0:T(8,128)(2,1)} %get-tuple-element.18.refs_0_, bf16[48,256]{1,0:T(8,128)(2,1)} %get-tuple-element.19.refs_1_, ...), custom_call_target="tpu_custom_call" | custom-call | tf_op jit(solution)/shard_map/pallas_call | solution.py:778

commit v5 on v4

--- a/solution.py
+++ b/solution.py
@@ -354,12 +354,12 @@
     for t in range(5, 8):
         for n in range(2):
             first_hop(t, n).start()
-    for t in range(1, 4):
-        arrive(t)
-
+    arrive(1)
+    arrive(2)
     for part in range(2):
         for n in range(2):
             exchange(part, n).start()
+    arrive(3)
 
     for load in loads[2 + 2 * heads : 2 + 4 * heads] + loads[3 + 4 * heads :]:
         load.wait()

time: 72.2 us -> 71.3 us (0.988); the launches traced: 70.8 us -> 70.8 us
  no operation moved by 1% of the time
where the time goes in v5:
time: 71.3 us; the launch traced here: 70.8 us
  Pallas kernels  70.1 us (98%)
    pallas_call x1, Pallas kernels, shards(): pl.pallas_call(body, out_shape=shapes, in_specs=[hbm] * 5 + [vmem] * 2 +...  67.8 us
    pallas_call x1, Pallas kernels, shards(): pl.pallas_call(hand_on, out_shape=shapes, in_specs=[vmem] * 6, out_specs=...  2.32 us

profile of v5, /device:TPU:0, one launch (start us, length us, event | category | flops | bytes accessed | tf_op | source)
XLA Modules:
  0.0 70.8 jit_solution(13794211197532483305)
XLA Ops:
  0.6 67.8 %shard_map.145 = (bf16[384,512]{1,0:T(8,128)(2,1)}, bf16[48,256]{1,0:T(8,128)(2,1)}, bf16[48,256]{1,0:T(8,128)(2,1)}, f32[8,128]{1,0:T(8,128)}, bf16[128,1536]{1,0:T(8,128)(2,1)}, /*index=5*/bf16[128,1536]{1,0:T(8,128)(2,1)}) custom-call(bf16[384,512]{1,0:T(8,128)(2,1)} %q_ref.1, bf16[384,256]{1,0:T(8,128)(2,1)} %k_ref.1, bf16[384,256]{1,0:T(8,128)(2,1)} %v_ref.1, ...), custom_call_target="tpu_custom_call" | custom-call | tf_op jit(solution)/shard_map/pallas_call | solution.py:710
  68.4 2.3 %shard_map.146 = (bf16[384,512]{1,0:T(8,128)(2,1)}, bf16[48,256]{1,0:T(8,128)(2,1)}, bf16[48,256]{1,0:T(8,128)(2,1)}, f32[8,128]{1,0:T(8,128)}, bf16[128,1536]{1,0:T(8,128)(2,1)}, /*index=5*/bf16[128,1536]{1,0:T(8,128)(2,1)}) custom-call(bf16[384,512]{1,0:T(8,128)(2,1)} %get-tuple-element.18.refs_0_, bf16[48,256]{1,0:T(8,128)(2,1)} %get-tuple-element.19.refs_1_, ...), custom_call_target="tpu_custom_call" | custom-call | tf_op jit(solution)/shard_map/pallas_call | solution.py:778

commit v6 on v5

--- a/solution.py
+++ b/solution.py
@@ -509,21 +509,19 @@
         return carry
 
     lax.fori_loop(0, 8, second_step, 0)
-    for s in range(1, -1, -1):
-        dqs[s] = (dq_acc[s] * SCALE).T.astype(jnp.bfloat16)
-        if s == 1:
-            d_copies = [
-                remote(
-                    dqs.at[1, pl.ds(h * sub, sub), :],
-                    dq_ref.at[pl.ds(sub, sub), pl.ds(h * HEAD, HEAD)],
-                    d_sem.at[0, h],
-                    d_sem.at[1, h],
-                    partner,
-                )
-                for h in range(heads)
-            ]
-            for copy in d_copies:
-                copy.start()
+    dqs[1] = (dq_acc[1] * SCALE).T.astype(jnp.bfloat16)
+    d_copies = [
+        remote(
+            dqs.at[1, pl.ds(h * sub, sub), :],
+            dq_ref.at[pl.ds(sub, sub), pl.ds(h * HEAD, HEAD)],
+            d_sem.at[0, h],
+            d_sem.at[1, h],
+            partner,
+        )
+        for h in range(heads)
+    ]
+    for copy in d_copies:
+        copy.start()
     after_merge(6)
     after_mate(4)
     outs = []
@@ -532,11 +530,6 @@
         copy = pltpu.make_async_copy(src, dst, out_sem.at[len(outs)])
         copy.start()
         outs.append(copy)
-
-    for h in range(heads):
-        store(
-            dqs.at[0, pl.ds(h * sub, sub), :], dq_ref.at[pl.ds(0, sub), pl.ds(h * HEAD, HEAD)]
-        )
 
     for copy in a_copies:
         copy.wait()
@@ -564,6 +557,11 @@
         return score + jnp.sum(act * back, axis=1, keepdims=True)
 
     after_merge(7)
+    dqs[0] = (dq_acc[0] * SCALE).T.astype(jnp.bfloat16)
+    for h in range(heads):
+        store(
+            dqs.at[0, pl.ds(h * sub, sub), :], dq_ref.at[pl.ds(0, sub), pl.ds(h * HEAD, HEAD)]
+        )
     score = lax.fori_loop(0, 2, expert_step, jnp.zeros((slots, 1), jnp.float32))
     cross()
     after_mate(5)

time: 71.3 us -> 71.3 us (level)
  no operation moved by 1% of the time
where the time goes in v6:
time: 71.3 us; the launch traced here: 70.9 us
  Pallas kernels  70.2 us (98%)
    pallas_call x1, Pallas kernels, shards(): pl.pallas_call(body, out_shape=shapes, in_specs=[hbm] * 5 + [vmem] * 2 +...  67.9 us
    pallas_call x1, Pallas kernels, shards(): pl.pallas_call(hand_on, out_shape=shapes, in_specs=[vmem] * 6, out_specs=...  2.32 us

profile of v6, /device:TPU:0, one launch (start us, length us, event | category | flops | bytes accessed | tf_op | source)
XLA Modules:
  0.0 70.9 jit_solution(9166824278856664927)
XLA Ops:
  0.6 67.9 %shard_map.145 = (bf16[384,512]{1,0:T(8,128)(2,1)}, bf16[48,256]{1,0:T(8,128)(2,1)}, bf16[48,256]{1,0:T(8,128)(2,1)}, f32[8,128]{1,0:T(8,128)}, bf16[128,1536]{1,0:T(8,128)(2,1)}, /*index=5*/bf16[128,1536]{1,0:T(8,128)(2,1)}) custom-call(bf16[384,512]{1,0:T(8,128)(2,1)} %q_ref.1, bf16[384,256]{1,0:T(8,128)(2,1)} %k_ref.1, bf16[384,256]{1,0:T(8,128)(2,1)} %v_ref.1, ...), custom_call_target="tpu_custom_call" | custom-call | tf_op jit(solution)/shard_map/pallas_call | solution.py:708
  68.6 2.3 %shard_map.146 = (bf16[384,512]{1,0:T(8,128)(2,1)}, bf16[48,256]{1,0:T(8,128)(2,1)}, bf16[48,256]{1,0:T(8,128)(2,1)}, f32[8,128]{1,0:T(8,128)}, bf16[128,1536]{1,0:T(8,128)(2,1)}, /*index=5*/bf16[128,1536]{1,0:T(8,128)(2,1)}) custom-call(bf16[384,512]{1,0:T(8,128)(2,1)} %get-tuple-element.18.refs_0_, bf16[48,256]{1,0:T(8,128)(2,1)} %get-tuple-element.19.refs_1_, ...), custom_call_target="tpu_custom_call" | custom-call | tf_op jit(solution)/shard_map/pallas_call | solution.py:776
